TPU v7x, 32 devices: a whole 2x2x4 slice. The times are simulated.
32 devices in a mesh: groups: 2 (over y), dp: 4 (over z), tensor: 4 (over x, core).
Axes of the slice: x: 2, y: 2, z: 4, core: 2. Of those that a mesh axis runs over, the one named last changes fastest.
Arguments:
- patches: bfloat16 [8192, 1280], P(('groups', 'dp')), parts along dimension 0, may hold values from -64 to 64
- grids: int32 [8, 2], P(('groups', 'dp')), parts along dimension 0, may hold values from 16 to 32, as said below
- dest: int32 [8, 256], P(('groups', 'dp')), parts along dimension 0, may hold values from 0 to 1535, as said below
- norm_gain: float32 [1280], replicated, may hold values from 0.1 to 1.9
- qkv_weight: bfloat16 [3, 1280, 1280], P(None, None, 'tensor'), may hold values from -8 to 8
- qkv_bias: float32 [3, 1280], P(None, 'tensor'), may hold values from -3 to 3
- proj_weight: bfloat16 [1280, 1280], P('tensor'), may hold values from -0.15625 to 0.15625
- proj_bias: float32 [1280], replicated, may hold values from -3 to 3
- merge_gain: float32 [1280], replicated, may hold values from 0.1 to 1.9
- w_first: bfloat16 [5120, 5120], P('dp', 'tensor'), may hold values from -0.078125 to 0.078125
- b_first: float32 [5120], P('tensor'), may hold values from -3 to 3
- w_second: bfloat16 [5120, 8192], P('tensor', 'dp'), may hold values from -0.078125 to 0.078125
- b_second: float32 [8192], P('tensor'), may hold values from -3 to 3
- text_embed: bfloat16 [3072, 8192], P(('groups', 'dp'), 'tensor'), parts along dimension 0, may hold values from -6 to 6
Outputs:
- sequence: bfloat16 [3072, 8192], P(('groups', 'dp'), 'tensor'), parts along dimension 0
There are 2 independent parts, one for each index of `groups`. A program takes and returns all parts, laid end to end along the dimension named above; an argument that names none is the same for every part. Nothing has to cross between parts.
Inputs may be any that keep to these rules, and one draw needn't show every extreme that they name: `grids`: both sides of every grid are even, at least 16 and at most 32; in each part along `groups`, the first image (the one on dp index 0) has the full 32 x 32 grid. The rows dest[i, j] with j < grids[i, 0] * grids[i, 1] / 4 are distinct over all images; the live rows of one image reach at most 64 rows in each aligned block of 384 sequence rows, and exactly that many for a full grid.
All inputs are finite; a program needn't handle non-finite values.
Results may differ from a plain program's by a relative error of at most 0.014.
Values may be sent and summed in bfloat16 or wider, within the bound.
No kernel may reach another device: no remote copies, remote signals or barrier semaphores. Data moves between devices by JAX's collectives and lax.ppermute only.
A program may use at most 128 MiB of HBM per device.

v0:
```python
import functools
import math

import jax
import jax.numpy as jnp
from jax import lax
from jax.experimental import pallas as pl
from jax.experimental.pallas import tpu as pltpu
from jax.sharding import PartitionSpec as P

HEAD_DIM = 80
MERGE = 4
BATCHES = 4
LANES = 128
QUERY_ROWS = 512
VMEM_BYTES = 48 * 1024 * 1024
ATTEND_VMEM_BYTES = 60 * 1024 * 1024


def rms_scale(values, gain):
    return values * lax.rsqrt(jnp.mean(values * values, axis=-1, keepdims=True) + 1e-06) * gain


def dot32(a, b):
    return jnp.dot(a, b, preferred_element_type=jnp.float32)


def dot32t(a, b):
    return lax.dot_general(a, b, (((1,), (1,)), ((), ())), preferred_element_type=jnp.float32)


def swap(x, axis, k):
    n = lax.axis_size(axis)
    return lax.ppermute(x, axis, [(a, a ^ k) for a in range(n)])


def gather_low(x, axis, count):
    blocks = {0: x}
    step = count // 2
    while step:
        for k in list(blocks):
            blocks[k | step] = swap(blocks[k], axis, step)
        step //= 2
    return [blocks[k] for k in range(count)]


def add16(a, b):
    return (a.astype(jnp.float32) + b.astype(jnp.float32)).astype(jnp.bfloat16)


def pick(x, at):
    return lax.dynamic_index_in_dim(x, at, 0, keepdims=False)


def line_sums(streams, axis, finish):
    n = lax.axis_size(axis)
    here = lax.axis_index(axis)
    blocks = streams[0][0].shape[0]
    steps = ((lambda a: (a, a + 1)), (lambda a: (n - 1 - a, n - 2 - a)))
    sent = [[[] for _ in steps] for _ in streams]
    came = [[[] for _ in steps] for _ in streams]
    results, waits = [], {}
    for step in range(n + blocks - 1):
        for s, terms in enumerate(streams):
            for w, step_to in enumerate(steps):
                value = terms[w][step % blocks]
                if step:
                    value = add16(value, came[s][w][-1])
                sent[s][w].append(value)
                if s and step in waits:
                    value, _ = lax.optimization_barrier((value, waits[step]))
                pairs = [step_to(a) for a in range(n - 1) if 0 <= step - a < blocks]
                if pairs:
                    came[s][w].append(lax.ppermute(value, axis, pairs))
        done = step - (n - 1)
        if done >= 0:
            sums = []
            for s in range(len(streams)):
                up, down = sent[s][0], came[s][1]
                below, above = up[done + n - 1], jnp.zeros_like(up[0])
                for place in range(n - 1):
                    below = jnp.where(here == place, up[done + place], below)
                    above = jnp.where(here == place, down[done + n - 2 - place], above)
                sums.append(below.astype(jnp.float32) + above.astype(jnp.float32))
            after = came[0][0][done + n - 1] if done + n - 1 < len(came[0][0]) else None
            waits[done + n], result = finish(done, sums, after, results)
            results.append(result)
    return results


def slots(target, seq_rows, shards, each):
    shard = jnp.where(target >= 0, target // seq_rows, shards)
    same = shard[..., :, None] == shard[..., None, :]
    earlier = each[None, :] < each[:, None]
    rank = jnp.sum((same & earlier).astype(jnp.int32), axis=-1)
    return shard, rank


def attend_kernel(grid_ref, x_hbm, gain_ref, w_hbm, b_ref, *rest):
    outs, scratch = rest[:-10], rest[-10:]
    x_ref, w_ref, n_ref, pad_ref, bias_ref, q_ref, k_ref, v_ref, att_ref, sems = scratch
    load_w = pltpu.make_async_copy(w_hbm, w_ref, sems.at[0])
    load_x = pltpu.make_async_copy(x_hbm, x_ref, sems.at[1])
    load_w.start()
    load_x.start()
    rows = x_ref.shape[0]
    heads = w_ref.shape[1] // HEAD_DIM
    live = grid_ref[0, 0] * grid_ref[0, 1]
    tensor_at = lax.axis_index("tensor")
    lane = lax.broadcasted_iota(jnp.int32, (1, heads * LANES), 1) % LANES
    for j in range(3):
        bias_ref[j : j + 1, :] = jnp.where((lane == HEAD_DIM) & (j != 1), 1.0, 0.0)
        for h in range(heads):
            low, at = h * LANES, h * HEAD_DIM
            bias_ref[j : j + 1, low : low + HEAD_DIM] = b_ref[j : j + 1, at : at + HEAD_DIM]
            pad_ref[j, low + HEAD_DIM : low + LANES, :] = jnp.zeros(
                (LANES - HEAD_DIM, w_ref.shape[2]), jnp.bfloat16
            )
    load_w.wait()
    for j in range(3):
        for h in range(heads):
            low, at = h * LANES, h * HEAD_DIM
            pad_ref[j, low : low + HEAD_DIM, :] = w_ref[j, at : at + HEAD_DIM, :]
    load_x.wait()
    step = min(QUERY_ROWS, rows)
    scale = math.log2(math.e) / math.sqrt(HEAD_DIM)
    extra = lax.broadcasted_iota(jnp.int32, (step, heads * LANES), 1) % LANES == HEAD_DIM
    row = lax.broadcasted_iota(jnp.int32, (step, heads * LANES), 0)
    gain = gain_ref[...].reshape(1, -1)
    for at in range(0, rows, step):
        span = slice(at, at + step)
        normed = rms_scale(x_ref[span, :].astype(jnp.float32), gain)
        n_ref[span, :] = normed.astype(jnp.bfloat16)
        for j, ref in enumerate((q_ref, k_ref, v_ref)):
            out = dot32t(n_ref[span, :], pad_ref[j]) + bias_ref[j : j + 1, :]
            if j == 0:
                out = out * scale
            if j == 1:
                out = jnp.where(extra & (row + at >= live), -1e30, out)
            ref[span, :] = out.astype(jnp.bfloat16)
    for at in range(0, rows, step):
        span = slice(at, at + step)
        for h in range(heads):
            lanes = slice(h * LANES, (h + 1) * LANES)
            scores = dot32t(q_ref[span, lanes], k_ref[:, lanes])
            peak = jnp.max(scores, axis=-1, keepdims=True)
            weights = jnp.exp2(scores - peak).astype(jnp.bfloat16)
            mixed = dot32(weights, v_ref[:, lanes])
            mixed = mixed[:, :HEAD_DIM] / mixed[:, HEAD_DIM : HEAD_DIM + 1]
            att_ref[span, h * HEAD_DIM : (h + 1) * HEAD_DIM] = mixed.astype(jnp.bfloat16)
    quarter = rows // len(outs)
    stores = []
    for k, out_hbm in enumerate(outs):
        low = pl.multiple_of((tensor_at ^ k) * quarter, quarter)
        store = pltpu.make_async_copy(att_ref.at[pl.ds(low, quarter)], out_hbm, sems.at[2 + k])
        store.start()
        stores.append(store)
    for store in stores:
        store.wait()


def vmem():
    return pl.BlockSpec(memory_space=pltpu.VMEM)


def smem():
    return pl.BlockSpec(memory_space=pltpu.SMEM)


def hbm():
    return pl.BlockSpec(memory_space=pltpu.HBM)


def anywhere():
    return pl.BlockSpec(memory_space=pl.ANY)


def bf16(*shape):
    return jax.ShapeDtypeStruct(shape, jnp.bfloat16)


def bf16_scratch(*shape):
    return pltpu.VMEM(shape, jnp.bfloat16)


def attend(grids, x, gain, w, b, parts):
    rows, width = x.shape
    cols = w.shape[1]
    padded = cols // HEAD_DIM * LANES
    return pl.pallas_call(
        attend_kernel,
        out_shape=[bf16(rows // parts, cols)] * parts,
        in_specs=[smem(), anywhere(), vmem(), anywhere(), vmem()],
        out_specs=[hbm()] * parts,
        scratch_shapes=[
            bf16_scratch(rows, width),
            bf16_scratch(3, cols, width),
            bf16_scratch(rows, width),
            bf16_scratch(3, padded, width),
            pltpu.VMEM((8, padded), jnp.float32),
            bf16_scratch(rows, padded),
            bf16_scratch(rows, padded),
            bf16_scratch(rows, padded),
            bf16_scratch(rows, cols),
            pltpu.SemaphoreType.DMA((2 + parts,)),
        ],
        compiler_params=pltpu.CompilerParams(vmem_limit_bytes=ATTEND_VMEM_BYTES),
        cost_estimate=pl.CostEstimate(
            flops=2 * rows * (3 * width * cols + 2 * rows * cols),
            bytes_accessed=2 * (2 * rows * width + 3 * width * cols),
            transcendentals=rows * rows * cols // HEAD_DIM,
        ),
    )(grids, x, gain, w, b)


def project_kernel(count, splits, x_hbm, bias_ref, gain_ref, *rest):
    blocks, weights, outs = rest[:count], rest[count : 2 * count], rest[2 * count : -5]
    x_ref, block_ref, weight_ref, out_ref, sems = rest[-5:]
    rows, size = x_ref.shape[0], out_ref.shape[1]
    low = pl.multiple_of(lax.axis_index("tensor") * rows, rows)
    loads = [pltpu.make_async_copy(x_hbm.at[pl.ds(low, rows)], x_ref, sems.at[0])]
    for k in range(count):
        loads.append(pltpu.make_async_copy(blocks[k], block_ref.at[k], sems.at[1 + 2 * k]))
        loads.append(pltpu.make_async_copy(weights[k], weight_ref.at[k], sems.at[2 + 2 * k]))
    for load in loads:
        load.start()
    loads[0].wait()
    summed = x_ref[...].astype(jnp.float32) + bias_ref[...].reshape(1, -1)
    for k in range(count):
        loads[1 + 2 * k].wait()
        loads[2 + 2 * k].wait()
        summed = summed + dot32(block_ref[k], weight_ref[k])
    merged = rms_scale(summed, gain_ref[...].reshape(1, -1)).astype(jnp.bfloat16)
    out_row = lax.broadcasted_iota(jnp.int32, (rows, rows), 0)
    row = lax.broadcasted_iota(jnp.int32, (rows, rows), 1)
    four = (out_row // size) ^ (lax.axis_index("dp") // splits)
    sort = (row == out_row % size * MERGE + four).astype(jnp.bfloat16)
    stores = []
    for k, out_hbm in enumerate(outs):
        out_ref[k] = dot32(sort[k * size : (k + 1) * size, :], merged).astype(jnp.bfloat16)
        store = pltpu.make_async_copy(out_ref.at[k], out_hbm, sems.at[k])
        store.start()
        stores.append(store)
    for store in stores:
        store.wait()


def project(x, bias, gain, blocks, weights, splits):
    rows, cols = blocks[0].shape
    width = x.shape[1]
    count = len(blocks)
    return pl.pallas_call(
        functools.partial(project_kernel, count, splits),
        out_shape=[bf16(rows // MERGE, width)] * MERGE,
        in_specs=[anywhere(), vmem(), vmem()] + [anywhere()] * (2 * count),
        out_specs=[hbm()] * MERGE,
        scratch_shapes=[
            bf16_scratch(rows, width),
            bf16_scratch(count, rows, cols),
            bf16_scratch(count, cols, width),
            bf16_scratch(MERGE, rows // MERGE, width),
            pltpu.SemaphoreType.DMA((max(MERGE, 1 + 2 * count),)),
        ],
        compiler_params=pltpu.CompilerParams(vmem_limit_bytes=VMEM_BYTES),
        cost_estimate=pl.CostEstimate(
            flops=2 * rows * width * width,
            bytes_accessed=2 * width * width + 6 * rows * width,
            transcendentals=rows,
        ),
    )(x, bias, gain, *blocks, *weights)


def first_kernel(groups, batches, images, w_ref, *rest):
    blocks, (up_ref, down_ref), (cat_ref, sems) = rest[:-4], rest[-4:-2], rest[-2:]
    count = len(blocks) // groups
    size = cat_ref.shape[0] // len(blocks)
    here, line = lax.axis_index("dp"), lax.axis_size("dp")
    loads = []
    for g in range(groups):
        for j in range(count):
            image = j ^ (here % images) if images > 1 else j
            low = (g * count + image) * size
            low = pl.multiple_of(low, size) if images > 1 else low
            place = cat_ref.at[pl.ds(low, size)]
            k = g * count + j
            loads.append(pltpu.make_async_copy(blocks[k], place, sems.at[k]))
            loads[-1].start()
    for load in loads:
        load.wait()
    rows = count // batches * size
    for g in range(groups):
        low = g * count * size
        out = dot32(cat_ref[low : low + count * size, :], w_ref[...]).astype(jnp.bfloat16)
        for j in range(batches):
            batch = j ^ (here // images)
            part = out[j * rows : (j + 1) * rows]
            up_ref[(batch + here) % batches, g] = part
            down_ref[(batch + line - 1 - here) % batches, g] = part


def first(groups, batches, w):
    count = len(groups[0])
    blocks = [block for group in groups for block in group]
    rows, depth = blocks[0].shape
    images = count // batches
    out = bf16(batches, len(groups), images * rows, w.shape[1])
    return pl.pallas_call(
        functools.partial(first_kernel, len(groups), batches, images),
        out_shape=[out, out],
        in_specs=[vmem()] + [anywhere()] * len(blocks),
        out_specs=[vmem(), vmem()],
        scratch_shapes=[
            bf16_scratch(rows * len(blocks), depth),
            pltpu.SemaphoreType.DMA((len(blocks),)),
        ],
        compiler_params=pltpu.CompilerParams(vmem_limit_bytes=VMEM_BYTES // 2),
        cost_estimate=pl.CostEstimate(
            flops=2 * rows * len(blocks) * depth * w.shape[1],
            bytes_accessed=2 * depth * w.shape[1] + 6 * rows * len(blocks) * depth,
            transcendentals=0,
        ),
    )(w, *blocks)


def second_kernel(count, bias_ref, goes_ref, w_hbm, *rest):
    totals, (send_ref, keep_ref), (w_ref, h_ref, sem) = rest[:count], rest[count:-3], rest[-3:]
    load = pltpu.make_async_copy(w_hbm, w_ref, sem)
    load.start()
    rows = totals[0].shape[0]
    bias = bias_ref[...].reshape(1, -1)
    for at, total in enumerate(totals):
        value = total[...] + bias
        value = 0.5 * value * (1.0 + lax.erf(value * math.sqrt(0.5)))
        h_ref[at * rows : (at + 1) * rows, :] = value.astype(jnp.bfloat16)
    half = send_ref.shape[0]
    index = lax.broadcasted_iota(jnp.int32, (half, 2 * half), 0)
    load.wait()
    for low, out_ref in ((half, send_ref), (0, keep_ref)):
        sort = (index + low == goes_ref[...]).astype(jnp.bfloat16)
        moved = dot32(sort, h_ref[...]).astype(jnp.bfloat16)
        out_ref[...] = dot32(moved, w_ref[...]).astype(jnp.bfloat16)


def second(totals, bias, goes, w):
    rows, width = totals[0].shape
    count = len(totals)
    out = bf16(rows * count // 2, w.shape[1])
    return pl.pallas_call(
        functools.partial(second_kernel, count),
        out_shape=[out, out],
        in_specs=[vmem(), vmem(), anywhere()] + [vmem()] * count,
        out_specs=[vmem(), vmem()],
        scratch_shapes=[
            bf16_scratch(*w.shape),
            bf16_scratch(rows * count, width),
            pltpu.SemaphoreType.DMA,
        ],
        compiler_params=pltpu.CompilerParams(vmem_limit_bytes=VMEM_BYTES),
        cost_estimate=pl.CostEstimate(
            flops=2 * rows * count * width * w.shape[1],
            bytes_accessed=2 * w.shape[0] * w.shape[1],
            transcendentals=rows * count * width,
        ),
    )(bias, goes, w, *totals)


def local(
    patches,
    grids,
    dest,
    norm_gain,
    qkv_weight,
    qkv_bias,
    proj_weight,
    proj_bias,
    merge_gain,
    w_first,
    b_first,
    w_second,
    b_second,
    text_embed,
):
    dps, tensors = lax.axis_size("dp"), lax.axis_size("tensor")
    tensor_at, dp_at = lax.axis_index("tensor"), lax.axis_index("dp")
    rows, width = patches.shape
    merged = dest.shape[1]
    seq_rows = text_embed.shape[0]
    cap = merged // dps
    part = cap // tensors

    proj_high = {0: proj_weight, tensors // 2: swap(proj_weight, "tensor", tensors // 2)}
    batches = min(dps, BATCHES)
    images = dps // batches
    blocks = attend(
        grids, patches, norm_gain, jnp.swapaxes(qkv_weight, 1, 2), qkv_bias, tensors
    )
    def places(after):
        early = (grids, dest, dp_at, tensor_at, jnp.arange(merged, dtype=jnp.int32))
        (sides, rows_to, here, there, each), _ = lax.optimization_barrier((early, after))
        live = sides[0, 0] * sides[0, 1]
        target = jnp.where(each * MERGE < live, rows_to[0], -1)
        targets = jnp.stack([swap(target, "dp", j) if j else target for j in range(dps)])
        targets = targets[jnp.arange(dps) ^ here]
        shard, rank = slots(targets, seq_rows, dps, each)
        quarter = (rank // part) ^ there
        bits = tensors.bit_length() - 1
        quarter = sum(((quarter >> k) & 1) << (bits - 1 - k) for k in range(bits))
        goes = (quarter * dps + shard) * part + rank % part
        image = jnp.arange(dps)[:, None] % images
        goes = jnp.where(targets >= 0, goes * images + image, -1)
        goes = goes.reshape(batches, images, tensors, merged // tensors).transpose(0, 2, 1, 3)
        goes = goes[:, jnp.arange(tensors) ^ there].reshape(batches, 1, images * merged)
        slot_rows = jnp.sum(
            jnp.where(
                (shard == here)[:, None, :]
                & (rank[:, None, :] == jnp.arange(cap)[None, :, None]),
                targets[:, None, :] % seq_rows + 1,
                0,
            ),
            axis=-1,
        )
        slot_rows = slot_rows.reshape(batches, images, tensors, part).transpose(2, 0, 3, 1) - 1
        slot_rows = slot_rows[jnp.arange(tensors) ^ there].reshape(1, -1)
        rows_out = jnp.arange(seq_rows, dtype=jnp.int32)[:, None]
        return goes, (rows_out == slot_rows).astype(jnp.bfloat16)

    blocks, proj_high = lax.optimization_barrier((list(blocks), proj_high))
    goes, hit = places(blocks[0])
    blocks = [swap(block, "tensor", k) if k else block for k, block in enumerate(blocks)]
    proj_blocks = {}
    for k, high in proj_high.items():
        for j, block in enumerate(gather_low(high, "tensor", tensors // 2)):
            proj_blocks[k | j] = block
    proj_blocks = [proj_blocks[k] for k in range(tensors)]
    proj_bias, goes, hit = lax.optimization_barrier((proj_bias, goes, hit))
    piece = w_first.shape[0]
    splits = width // piece
    merged_in = project(patches, proj_bias, merge_gain, blocks, proj_blocks, splits)

    near, far = ([[] for _ in range(tensors // 2)] for _ in range(2))
    for j in range(dps):
        block = merged_in[j // splits]
        if splits > 1:
            at = ((dp_at ^ j) % splits) * piece
            block = lax.dynamic_slice_in_dim(block, at, piece, 1)
        if j:
            block = swap(block, "dp", j)
        for k, line in enumerate(gather_low(block, "tensor", tensors // 2)):
            near[k].append(line)
        high = swap(block, "tensor", tensors // 2)
        for k, line in enumerate(gather_low(high, "tensor", tensors // 2)):
            far[k].append(line)
    streams = [first(near, batches, w_first), first(far, batches, w_first)]

    columns = w_second.shape[1]
    shares = dps // tensors

    def to_shards(members):
        members = jnp.stack(members, axis=1)
        blocks = []
        for j in range(dps):
            moved = pick(members, dp_at ^ j)
            blocks.append(swap(moved, "dp", j) if j else moved)
        return blocks

    arrived = []

    def finish(batch, sums, after, results):
        if batch == batches - 1:
            arrived.append(to_shards(results[: batches - 2]))
            after = arrived[0][1]
        if after is not None:
            sums, _ = lax.optimization_barrier((sums, after))
        rows_in = [part.reshape(-1, w_second.shape[0]) for part in sums]
        send, block = second(rows_in, b_first, goes[batch], w_second)
        wait = send
        block = add16(block, swap(send, "tensor", 1))
        step = 2
        while step < tensors:
            half = block.shape[0] // 2
            block = add16(block[:half], swap(block[half:], "tensor", step))
            step *= 2
        return wait, block.reshape(dps, part * images, columns)

    held = line_sums(streams, "dp", finish)
    for block in held[batches - 2 :]:
        arrived.append(to_shards([block]))
    arrived = jnp.concatenate([jnp.stack(blocks) for blocks in arrived], axis=1)
    arrived = arrived.reshape(tensors, shares, -1, columns)
    visual = []
    for k in range(tensors):
        moved = pick(arrived, (tensor_at ^ k) ^ (dp_at // shares))
        moved = swap(moved, "tensor", k) if k else moved
        if shares > 1:
            moved = jnp.concatenate(
                [pick(moved, (dp_at % shares) ^ j) for j in range(shares)], axis=-1
            )
        visual.append(moved.reshape(-1, shares * columns))
    visual = jnp.concatenate(visual, axis=0)

    covered = jnp.sum(hit, axis=1, keepdims=True, dtype=jnp.float32) > 0
    placed = dot32(hit, visual) + b_second
    return jnp.where(covered, placed.astype(jnp.bfloat16), text_embed)


def solution(mesh):
    in_specs = (
        P(("groups", "dp"), None),
        P(("groups", "dp"), None),
        P(("groups", "dp"), None),
        P(),
        P(None, None, "tensor"),
        P(None, "tensor"),
        P("tensor", None),
        P(),
        P(),
        P("dp", "tensor"),
        P("tensor"),
        P("tensor", "dp"),
        P("tensor"),
        P(("groups", "dp"), "tensor"),
    )
    out_specs = P(("groups", "dp"), "tensor")
    return jax.shard_map(local, mesh=mesh, in_specs=in_specs, out_specs=out_specs, check_vma=False)
```

profile of v0, /device:TPU:0, one launch (start us, length us, event | category | flops | bytes accessed | tf_op | source)
XLA Modules:
  0.0 228.4 jit_solution(9418874436684355366)
XLA Ops:
  3.0 14.2 %shard_map.136 = (bf16[256,320]{1,0:T(8,128)(2,1)}, bf16[256,320]{1,0:T(8,128)(2,1)}, bf16[256,320]{1,0:T(8,128)(2,1)}, bf16[256,320]{1,0:T(8,128)(2,1)}) custom-call(s32[1,2]{1,0:T(1,128)} %grid_ref.1, bf16[1024,1280]{1,0:T(8,128)(2,1)} %x_hbm.3, f32[1280]{0:T(1024)} %gain_ref.2, bf16[3,320,1280]{2,1,0:T(8,128)(2,1)} %bitcast.186, f32[3,320]{1,0:T(4,128)} %b_ref.1), custom_call_target="tpu_custom_call" | custom-call | flops 3858759680 | bytes 7700480 | tf_op jit(solution)/shard_map/pallas_call | solution.py:190
  17.1 4.2 %collective-permute-done.rest_6_ = bf16[320,1280]{1,0:T(8,128)(2,1)S(1)} collective-permute-done((bf16[320,1280]{1,0:T(8,128)(2,1)}, bf16[320,1280]{1,0:T(8,128)(2,1)S(1)}, u32[]{:S(2)}, u32[]{:S(2)}) %collective-permute-start) | collective-permute-done | bytes 819232 | tf_op jit(solution)/shard_map/ppermute | solution.py:34
  23.3 3.9 %collective-permute-start.3 = (s32[256]{0:T(256)S(1)}, s32[256]{0:T(256)S(1)}, u32[]{:S(2)}, u32[]{:S(2)}) collective-permute-start(s32[256]{0:T(256)S(1)} %compare_select_fusion.2), channel_id=1, source_target_pairs={{0,12},{4,8},{8,4},{12,0},{1,13},{5,9},{9,5},{13,1},{2,14},{6,10},... | collective-permute-start | bytes 3080 | tf_op jit(solution)/shard_map/ppermute | solution.py:34
  41.0 5.0 %shard_map.137 = (bf16[64,1280]{1,0:T(8,128)(2,1)S(1)}, bf16[64,1280]{1,0:T(8,128)(2,1)}, bf16[64,1280]{1,0:T(8,128)(2,1)}, bf16[64,1280]{1,0:T(8,128)(2,1)}) custom-call(bf16[1024,1280]{1,0:T(8,128)(2,1)} %x_hbm.3, f32[1280]{0:T(1024)S(1)} %copy-done.3, f32[1280]{0:T(1024)S(1)} %copy-done.4, bf16[256,320]{1,0:T(8,128)(2,1)S(1)} %copy-done.1, ...), custom_call_target="tpu_custom_call" | custom-call | flops 838860800 | bytes 5242880 | tf_op jit(solution)/shard_map/pallas_call | solution.py:252
  56.4 6.9 %collective-permute-done.10.rest_2_ = bf16[64,1280]{1,0:T(8,128)(2,1)S(1)} collective-permute-done((bf16[64,1280]{1,0:T(8,128)(2,1)}, bf16[64,1280]{1,0:T(8,128)(2,1)S(1)}, u32[]{:S(2)}, u32[]{:S(2)}) %collective-permute-start.10) | collective-permute-done | bytes 163872 | tf_op jit(solution)/shard_map/ppermute | solution.py:34
  70.3 3.7 %shard_map.138 = (bf16[4,2,64,1280]{3,2,1,0:T(8,128)(2,1)S(1)}, bf16[4,2,64,1280]{3,2,1,0:T(8,128)(2,1)S(1)}) custom-call(bf16[1280,1280]{1,0:T(8,128)(2,1)S(1)} %copy-done.5, bf16[64,1280]{1,0:T(8,128)(2,1)S(1)} %copy-done.8, bf16[64,1280]{1,0:T(8,128)(2,1)S(1)} %collective-permute-done.9.rest_1_, bf16[64,1280]{1,0:T(8,128)(2,1)S(1)} %collective-permute-done.10.rest_2_, ...), custom_call_target="tpu_custom_call" | custom-call | flops 1677721600 | bytes 7208960 | tf_op jit(solution)/shard_map/pallas_call | solution.py:307
  77.1 5.3 %collective-permute-start.16 = (bf16[2,64,1280]{2,1,0:T(8,128)(2,1)S(1)}, bf16[2,64,1280]{2,1,0:T(8,128)(2,1)S(1)}, u32[]{:S(2)}, u32[]{:S(2)}) collective-permute-start(bf16[2,64,1280]{2,1,0:T(8,128)(2,1)S(1)} %slice_bitcast_fusion.3), channel_id=1, source_target_pairs={{0,4},{1,5},{2,6},{3,7},{16,20},{17,21},{18,22},{19,23}} | collective-permute-start | bytes 983048 | tf_op jit(solution)/shard_map/ppermute | solution.py:74
  83.2 3.7 %shard_map.139 = (bf16[4,2,64,1280]{3,2,1,0:T(8,128)(2,1)S(1)}, bf16[4,2,64,1280]{3,2,1,0:T(8,128)(2,1)S(1)}) custom-call(bf16[1280,1280]{1,0:T(8,128)(2,1)S(1)} %copy-done.6, bf16[64,1280]{1,0:T(8,128)(2,1)S(1)} %collective-permute-done.22.rest_0_, bf16[64,1280]{1,0:T(8,128)(2,1)S(1)} %collective-permute-done.23.rest_1_, ...), custom_call_target="tpu_custom_call" | custom-call | flops 1677721600 | bytes 7208960 | tf_op jit(solution)/shard_map/pallas_call | solution.py:307
  90.5 4.4 %collective-permute-start.17 = (bf16[2,64,1280]{2,1,0:T(8,128)(2,1)S(1)}, bf16[2,64,1280]{2,1,0:T(8,128)(2,1)S(1)}, u32[]{:S(2)}, u32[]{:S(2)}) collective-permute-start(bf16[2,64,1280]{2,1,0:T(8,128)(2,1)S(1)} %fusion.8), channel_id=1, source_target_pairs={{0,4},{4,8},{1,5},{5,9},{2,6},{6,10},{3,7},{7,11},{16,20},{20,24},... | collective-permute-start | bytes 983048 | tf_op jit(solution)/shard_map/ppermute | solution.py:74
  97.5 4.4 %collective-permute-start.31 = (bf16[2,64,1280]{2,1,0:T(8,128)(2,1)S(1)}, bf16[2,64,1280]{2,1,0:T(8,128)(2,1)S(1)}, u32[]{:S(2)}, u32[]{:S(2)}) collective-permute-start(bf16[2,64,1280]{2,1,0:T(8,128)(2,1)S(1)} %fusion.10), channel_id=1, source_target_pairs={{0,4},{4,8},{1,5},{5,9},{2,6},{6,10},{3,7},{7,11},{16,20},{20,24},... | collective-permute-start | bytes 983048 | tf_op jit(solution)/shard_map/ppermute | solution.py:74
  104.6 4.4 %collective-permute-start.18 = (bf16[2,64,1280]{2,1,0:T(8,128)(2,1)S(1)}, bf16[2,64,1280]{2,1,0:T(8,128)(2,1)S(1)}, u32[]{:S(2)}, u32[]{:S(2)}) collective-permute-start(bf16[2,64,1280]{2,1,0:T(8,128)(2,1)S(1)} %fusion.12), channel_id=1, source_target_pairs={{0,4},{4,8},{8,12},{1,5},{5,9},{9,13},{2,6},{6,10},{10,14},{3,7},{... | collective-permute-start | bytes 983048 | tf_op jit(solution)/shard_map/ppermute | solution.py:74
  111.6 4.4 %collective-permute-start.32 = (bf16[2,64,1280]{2,1,0:T(8,128)(2,1)S(1)}, bf16[2,64,1280]{2,1,0:T(8,128)(2,1)S(1)}, u32[]{:S(2)}, u32[]{:S(2)}) collective-permute-start(bf16[2,64,1280]{2,1,0:T(8,128)(2,1)S(1)} %fusion.16), channel_id=1, source_target_pairs={{0,4},{4,8},{8,12},{1,5},{5,9},{9,13},{2,6},{6,10},{10,14},{3,7},{... | collective-permute-start | bytes 983048 | tf_op jit(solution)/shard_map/ppermute | solution.py:74
  121.4 4.6 %collective-permute-start.36 = (bf16[2,64,1280]{2,1,0:T(8,128)(2,1)S(1)}, bf16[2,64,1280]{2,1,0:T(8,128)(2,1)S(1)}, u32[]{:S(2)}, u32[]{:S(2)}) collective-permute-start(bf16[2,64,1280]{2,1,0:T(8,128)(2,1)S(1)} %get-tuple-element.108), channel_id=1, source_target_pairs={{0,4},{4,8},{8,12},{1,5},{5,9},{9,13},{2,6},{6,10},{10,14},{3,7},{... | collective-permute-start | bytes 983048 | tf_op jit(solution)/shard_map/ppermute | solution.py:74
  130.4 4.6 %collective-permute-start.40 = (bf16[2,64,1280]{2,1,0:T(8,128)(2,1)S(1)}, bf16[2,64,1280]{2,1,0:T(8,128)(2,1)S(1)}, u32[]{:S(2)}, u32[]{:S(2)}) collective-permute-start(bf16[2,64,1280]{2,1,0:T(8,128)(2,1)S(1)} %get-tuple-element.106), channel_id=1, source_target_pairs={{0,4},{4,8},{8,12},{1,5},{5,9},{9,13},{2,6},{6,10},{10,14},{3,7},{... | collective-permute-start | bytes 983048 | tf_op jit(solution)/shard_map/ppermute | solution.py:74
  138.3 4.3 %shard_map.140 = (bf16[128,2048]{1,0:T(8,128)(2,1)S(1)}, bf16[128,2048]{1,0:T(8,128)(2,1)S(1)}) custom-call(f32[1280]{0:T(1024)S(1)} %copy-done.2, s32[1,256]{1,0:T(1,128)S(1)} %get-tuple-element.136.goes_ref, bf16[1280,2048]{1,0:T(8,128)(2,1)} %w_hbm.7, f32[128,1280]{1,0:T(8,128)S(1)} %bitcast.158, f32[128,1280]{1,0:T(8,128)S(1)} %bitcast.160), custom_call_target="tpu_custom_call" | custom-call | flops 1342177280 | bytes 5242880 | tf_op jit(solution)/shard_map/pallas_call | solution.py:348
  150.2 4.3 %shard_map.141 = (bf16[128,2048]{1,0:T(8,128)(2,1)S(1)}, bf16[128,2048]{1,0:T(8,128)(2,1)S(1)}) custom-call(f32[1280]{0:T(1024)S(1)} %copy-done.2, s32[1,256]{1,0:T(1,128)S(1)} %get-tuple-element.135.goes_ref, bf16[1280,2048]{1,0:T(8,128)(2,1)} %w_hbm.7, f32[128,1280]{1,0:T(8,128)S(1)} %bitcast.156, f32[128,1280]{1,0:T(8,128)S(1)} %bitcast.159), custom_call_target="tpu_custom_call" | custom-call | flops 1342177280 | bytes 5242880 | tf_op jit(solution)/shard_map/pallas_call | solution.py:348
  154.5 4.4 %collective-permute-done.50 = bf16[2,64,1280]{2,1,0:T(8,128)(2,1)S(1)} collective-permute-done((bf16[2,64,1280]{2,1,0:T(8,128)(2,1)S(1)}, bf16[2,64,1280]{2,1,0:T(8,128)(2,1)S(1)}, u32[]{:S(2)}, u32[]{:S(2)}) %collective-permute-start.50) | collective-permute-done | bytes 327712 | tf_op jit(solution)/shard_map/ppermute | solution.py:74
  163.3 4.3 %shard_map.142 = (bf16[128,2048]{1,0:T(8,128)(2,1)S(1)}, bf16[128,2048]{1,0:T(8,128)(2,1)S(1)}) custom-call(f32[1280]{0:T(1024)S(1)} %copy-done.2, s32[1,256]{1,0:T(1,128)S(1)} %get-tuple-element.133.goes_ref, bf16[1280,2048]{1,0:T(8,128)(2,1)} %w_hbm.7, f32[128,1280]{1,0:T(8,128)S(1)} %bitcast.157, f32[128,1280]{1,0:T(8,128)S(1)} %bitcast.161), custom_call_target="tpu_custom_call" | custom-call | flops 1342177280 | bytes 5242880 | tf_op jit(solution)/shard_map/pallas_call | solution.py:348
  169.4 7.6 %collective-permute-done.44 = bf16[64,2048]{1,0:T(8,128)(2,1)S(1)} collective-permute-done((bf16[64,2048]{1,0:T(8,128)(2,1)S(1)}, bf16[64,2048]{1,0:T(8,128)(2,1)S(1)}, u32[]{:S(2)}, u32[]{:S(2)}) %collective-permute-start.44) | collective-permute-done | bytes 262176 | tf_op jit(solution)/shard_map/ppermute | solution.py:34
  183.2 4.3 %shard_map.143 = (bf16[128,2048]{1,0:T(8,128)(2,1)S(1)}, bf16[128,2048]{1,0:T(8,128)(2,1)S(1)}) custom-call(f32[1280]{0:T(1024)S(1)} %copy-done.2, s32[1,256]{1,0:T(1,128)S(1)} %get-tuple-element.134.goes_ref, bf16[1280,2048]{1,0:T(8,128)(2,1)} %w_hbm.7, f32[128,1280]{1,0:T(8,128)S(1)} %bitcast.155, f32[128,1280]{1,0:T(8,128)S(1)} %bitcast.162), custom_call_target="tpu_custom_call" | custom-call | flops 1342177280 | bytes 5242880 | tf_op jit(solution)/shard_map/pallas_call | solution.py:348
  194.9 5.3 %collective-permute-done.61 = bf16[64,2048]{1,0:T(8,128)(2,1)S(1)} collective-permute-done((bf16[64,2048]{1,0:T(8,128)(2,1)S(1)}, bf16[64,2048]{1,0:T(8,128)(2,1)S(1)}, u32[]{:S(2)}, u32[]{:S(2)}) %collective-permute-start.61) | collective-permute-done | bytes 262176 | tf_op jit(solution)/shard_map/ppermute | solution.py:34
  202.0 5.6 %collective-permute-start.63 = (bf16[1,16,2048]{2,1,0:T(8,128)(2,1)S(1)}, bf16[1,16,2048]{2,1,0:T(8,128)(2,1)S(1)}, u32[]{:S(2)}, u32[]{:S(2)}) collective-permute-start(bf16[1,16,2048]{2,1,0:T(8,128)(2,1)S(1)} %get-tuple-element.131), channel_id=1, source_target_pairs={{0,8},{4,12},{8,0},{12,4},{1,9},{5,13},{9,1},{13,5},{2,10},{6,14},... | collective-permute-start | bytes 196616 | tf_op jit(solution)/shard_map/ppermute | solution.py:34
  216.2 6.6 %collective-permute-done.67 = bf16[1,64,2048]{2,1,0:T(8,128)(2,1)S(1)} collective-permute-done((bf16[1,64,2048]{2,1,0:T(8,128)(2,1)S(1)}, bf16[1,64,2048]{2,1,0:T(8,128)(2,1)S(1)}, u32[]{:S(2)}, u32[]{:S(2)}) %collective-permute-start.67) | collective-permute-done | bytes 262176 | tf_op jit(solution)/shard_map/ppermute | solution.py:34
  222.8 3.9 %collective-permute-done.66 = bf16[1,64,2048]{2,1,0:T(8,128)(2,1)S(1)} collective-permute-done((bf16[1,64,2048]{2,1,0:T(8,128)(2,1)S(1)}, bf16[1,64,2048]{2,1,0:T(8,128)(2,1)S(1)}, u32[]{:S(2)}, u32[]{:S(2)}) %collective-permute-start.66) | collective-permute-done | bytes 262176 | tf_op jit(solution)/shard_map/ppermute | solution.py:34
  (218 shorter events, 101.9 us)
Async XLA Ops:
  0.0 21.4 %collective-permute-start = (bf16[320,1280]{1,0:T(8,128)(2,1)}, bf16[320,1280]{1,0:T(8,128)(2,1)S(1)}, u32[]{:S(2)}, u32[]{:S(2)}) collective-permute-start(bf16[320,1280]{1,0:T(8,128)(2,1)} %rest_4_), channel_id=1, source_target_pairs={{0,2},{1,3},{2,0},{3,1},{4,6},{5,7},{6,4},{7,5},{8,10},{9,11},{10,... | collective-permute-start | bytes 2457608 | tf_op jit(solution)/shard_map/ppermute | solution.py:34
  48.2 15.2 %collective-permute-start.10 = (bf16[64,1280]{1,0:T(8,128)(2,1)}, bf16[64,1280]{1,0:T(8,128)(2,1)S(1)}, u32[]{:S(2)}, u32[]{:S(2)}) collective-permute-start(bf16[64,1280]{1,0:T(8,128)(2,1)} %get-tuple-element.71), channel_id=1, source_target_pairs={{0,8},{4,12},{8,0},{12,4},{1,9},{5,13},{9,1},{13,5},{2,10},{6,14},... | collective-permute-start | bytes 491528 | tf_op jit(solution)/shard_map/ppermute | solution.py:34
  51.1 12.7 %collective-permute-start.22 = (bf16[64,1280]{1,0:T(8,128)(2,1)}, bf16[64,1280]{1,0:T(8,128)(2,1)S(1)}, u32[]{:S(2)}, u32[]{:S(2)}) collective-permute-start(bf16[64,1280]{1,0:T(8,128)(2,1)} %copy-done.7), channel_id=1, source_target_pairs={{0,2},{1,3},{2,0},{3,1},{4,6},{5,7},{6,4},{7,5},{8,10},{9,11},{10,... | collective-permute-start | bytes 491528 | tf_op jit(solution)/shard_map/ppermute | solution.py:34
  67.5 15.0 %collective-permute-start.26 = (bf16[64,1280]{1,0:T(8,128)(2,1)S(1)}, bf16[64,1280]{1,0:T(8,128)(2,1)S(1)}, u32[]{:S(2)}, u32[]{:S(2)}) collective-permute-start(bf16[64,1280]{1,0:T(8,128)(2,1)S(1)} %collective-permute-done.22.rest_0_), channel_id=1, source_target_pairs={{0,1},{1,0},{2,3},{3,2},{4,5},{5,4},{6,7},{7,6},{8,9},{9,8},{10,11... | collective-permute-start | bytes 491528 | tf_op jit(solution)/shard_map/ppermute | solution.py:34
  77.1 13.3 %collective-permute-start.16 = (bf16[2,64,1280]{2,1,0:T(8,128)(2,1)S(1)}, bf16[2,64,1280]{2,1,0:T(8,128)(2,1)S(1)}, u32[]{:S(2)}, u32[]{:S(2)}) collective-permute-start(bf16[2,64,1280]{2,1,0:T(8,128)(2,1)S(1)} %slice_bitcast_fusion.3), channel_id=1, source_target_pairs={{0,4},{1,5},{2,6},{3,7},{16,20},{17,21},{18,22},{19,23}} | collective-permute-start | bytes 983048 | tf_op jit(solution)/shard_map/ppermute | solution.py:74
  88.3 13.7 %collective-permute-start.33 = (bf16[2,64,1280]{2,1,0:T(8,128)(2,1)S(1)}, bf16[2,64,1280]{2,1,0:T(8,128)(2,1)S(1)}, u32[]{:S(2)}, u32[]{:S(2)}) collective-permute-start(bf16[2,64,1280]{2,1,0:T(8,128)(2,1)S(1)} %slice_bitcast_fusion), channel_id=1, source_target_pairs={{12,8},{13,9},{14,10},{15,11},{28,24},{29,25},{30,26},{31,27}} | collective-permute-start | bytes 983048 | tf_op jit(solution)/shard_map/ppermute | solution.py:74
  90.5 14.0 %collective-permute-start.17 = (bf16[2,64,1280]{2,1,0:T(8,128)(2,1)S(1)}, bf16[2,64,1280]{2,1,0:T(8,128)(2,1)S(1)}, u32[]{:S(2)}, u32[]{:S(2)}) collective-permute-start(bf16[2,64,1280]{2,1,0:T(8,128)(2,1)S(1)} %fusion.8), channel_id=1, source_target_pairs={{0,4},{4,8},{1,5},{5,9},{2,6},{6,10},{3,7},{7,11},{16,20},{20,24},... | collective-permute-start | bytes 983048 | tf_op jit(solution)/shard_map/ppermute | solution.py:74
  95.0 13.9 %collective-permute-start.20 = (bf16[2,64,1280]{2,1,0:T(8,128)(2,1)S(1)}, bf16[2,64,1280]{2,1,0:T(8,128)(2,1)S(1)}, u32[]{:S(2)}, u32[]{:S(2)}) collective-permute-start(bf16[2,64,1280]{2,1,0:T(8,128)(2,1)S(1)} %fusion.14), channel_id=1, source_target_pairs={{12,8},{8,4},{13,9},{9,5},{14,10},{10,6},{15,11},{11,7},{28,24},{2... | collective-permute-start | bytes 983048 | tf_op jit(solution)/shard_map/ppermute | solution.py:74
  97.5 14.0 %collective-permute-start.31 = (bf16[2,64,1280]{2,1,0:T(8,128)(2,1)S(1)}, bf16[2,64,1280]{2,1,0:T(8,128)(2,1)S(1)}, u32[]{:S(2)}, u32[]{:S(2)}) collective-permute-start(bf16[2,64,1280]{2,1,0:T(8,128)(2,1)S(1)} %fusion.10), channel_id=1, source_target_pairs={{0,4},{4,8},{1,5},{5,9},{2,6},{6,10},{3,7},{7,11},{16,20},{20,24},... | collective-permute-start | bytes 983048 | tf_op jit(solution)/shard_map/ppermute | solution.py:74
  102.1 13.9 %collective-permute-start.34 = (bf16[2,64,1280]{2,1,0:T(8,128)(2,1)S(1)}, bf16[2,64,1280]{2,1,0:T(8,128)(2,1)S(1)}, u32[]{:S(2)}, u32[]{:S(2)}) collective-permute-start(bf16[2,64,1280]{2,1,0:T(8,128)(2,1)S(1)} %fusion.18), channel_id=1, source_target_pairs={{12,8},{8,4},{13,9},{9,5},{14,10},{10,6},{15,11},{11,7},{28,24},{2... | collective-permute-start | bytes 983048 | tf_op jit(solution)/shard_map/ppermute | solution.py:74
  104.6 14.0 %collective-permute-start.18 = (bf16[2,64,1280]{2,1,0:T(8,128)(2,1)S(1)}, bf16[2,64,1280]{2,1,0:T(8,128)(2,1)S(1)}, u32[]{:S(2)}, u32[]{:S(2)}) collective-permute-start(bf16[2,64,1280]{2,1,0:T(8,128)(2,1)S(1)} %fusion.12), channel_id=1, source_target_pairs={{0,4},{4,8},{8,12},{1,5},{5,9},{9,13},{2,6},{6,10},{10,14},{3,7},{... | collective-permute-start | bytes 983048 | tf_op jit(solution)/shard_map/ppermute | solution.py:74
  111.6 14.4 %collective-permute-start.32 = (bf16[2,64,1280]{2,1,0:T(8,128)(2,1)S(1)}, bf16[2,64,1280]{2,1,0:T(8,128)(2,1)S(1)}, u32[]{:S(2)}, u32[]{:S(2)}) collective-permute-start(bf16[2,64,1280]{2,1,0:T(8,128)(2,1)S(1)} %fusion.16), channel_id=1, source_target_pairs={{0,4},{4,8},{8,12},{1,5},{5,9},{9,13},{2,6},{6,10},{10,14},{3,7},{... | collective-permute-start | bytes 983048 | tf_op jit(solution)/shard_map/ppermute | solution.py:74
  120.1 15.6 %collective-permute-start.39 = (bf16[2,64,1280]{2,1,0:T(8,128)(2,1)S(1)}, bf16[2,64,1280]{2,1,0:T(8,128)(2,1)S(1)}, u32[]{:S(2)}, u32[]{:S(2)}) collective-permute-start(bf16[2,64,1280]{2,1,0:T(8,128)(2,1)S(1)} %get-tuple-element.126), channel_id=1, source_target_pairs={{12,8},{8,4},{4,0},{13,9},{9,5},{5,1},{14,10},{10,6},{6,2},{15,11}... | collective-permute-start | bytes 983048 | tf_op jit(solution)/shard_map/ppermute | solution.py:74
  121.4 14.3 %collective-permute-start.36 = (bf16[2,64,1280]{2,1,0:T(8,128)(2,1)S(1)}, bf16[2,64,1280]{2,1,0:T(8,128)(2,1)S(1)}, u32[]{:S(2)}, u32[]{:S(2)}) collective-permute-start(bf16[2,64,1280]{2,1,0:T(8,128)(2,1)S(1)} %get-tuple-element.108), channel_id=1, source_target_pairs={{0,4},{4,8},{8,12},{1,5},{5,9},{9,13},{2,6},{6,10},{10,14},{3,7},{... | collective-permute-start | bytes 983048 | tf_op jit(solution)/shard_map/ppermute | solution.py:74
  129.1 13.6 %collective-permute-start.41 = (bf16[2,64,1280]{2,1,0:T(8,128)(2,1)S(1)}, bf16[2,64,1280]{2,1,0:T(8,128)(2,1)S(1)}, u32[]{:S(2)}, u32[]{:S(2)}) collective-permute-start(bf16[2,64,1280]{2,1,0:T(8,128)(2,1)S(1)} %get-tuple-element.123), channel_id=1, source_target_pairs={{12,8},{8,4},{4,0},{13,9},{9,5},{5,1},{14,10},{10,6},{6,2},{15,11}... | collective-permute-start | bytes 983048 | tf_op jit(solution)/shard_map/ppermute | solution.py:74
  142.6 17.4 %collective-permute-start.37 = (bf16[128,2048]{1,0:T(8,128)(2,1)S(1)}, bf16[128,2048]{1,0:T(8,128)(2,1)S(1)}, u32[]{:S(2)}, u32[]{:S(2)}) collective-permute-start(bf16[128,2048]{1,0:T(8,128)(2,1)S(1)} %get-tuple-element.80), channel_id=1, source_target_pairs={{0,1},{1,0},{2,3},{3,2},{4,5},{5,4},{6,7},{7,6},{8,9},{9,8},{10,11... | collective-permute-start | bytes 1572872 | tf_op jit(solution)/shard_map/ppermute | solution.py:34
  143.8 15.1 %collective-permute-start.50 = (bf16[2,64,1280]{2,1,0:T(8,128)(2,1)S(1)}, bf16[2,64,1280]{2,1,0:T(8,128)(2,1)S(1)}, u32[]{:S(2)}, u32[]{:S(2)}) collective-permute-start(bf16[2,64,1280]{2,1,0:T(8,128)(2,1)S(1)} %get-tuple-element.86), channel_id=1, source_target_pairs={{8,4},{4,0},{9,5},{5,1},{10,6},{6,2},{11,7},{7,3},{24,20},{20,16},... | collective-permute-start | bytes 983048 | tf_op jit(solution)/shard_map/ppermute | solution.py:74
  148.2 19.5 %collective-permute-start.57 = (bf16[2,64,1280]{2,1,0:T(8,128)(2,1)S(1)}, bf16[2,64,1280]{2,1,0:T(8,128)(2,1)S(1)}, u32[]{:S(2)}, u32[]{:S(2)}) collective-permute-start(bf16[2,64,1280]{2,1,0:T(8,128)(2,1)S(1)} %get-tuple-element.124), channel_id=1, source_target_pairs={{4,0},{5,1},{6,2},{7,3},{20,16},{21,17},{22,18},{23,19}} | collective-permute-start | bytes 983048 | tf_op jit(solution)/shard_map/ppermute | solution.py:74
  154.5 13.6 %collective-permute-start.43 = (bf16[128,2048]{1,0:T(8,128)(2,1)S(1)}, bf16[128,2048]{1,0:T(8,128)(2,1)S(1)}, u32[]{:S(2)}, u32[]{:S(2)}) collective-permute-start(bf16[128,2048]{1,0:T(8,128)(2,1)S(1)} %get-tuple-element.84), channel_id=1, source_target_pairs={{0,1},{1,0},{2,3},{3,2},{4,5},{5,4},{6,7},{7,6},{8,9},{9,8},{10,11... | collective-permute-start | bytes 1572872 | tf_op jit(solution)/shard_map/ppermute | solution.py:34
  159.3 21.3 %collective-permute-start.58 = (bf16[2,64,1280]{2,1,0:T(8,128)(2,1)S(1)}, bf16[2,64,1280]{2,1,0:T(8,128)(2,1)S(1)}, u32[]{:S(2)}, u32[]{:S(2)}) collective-permute-start(bf16[2,64,1280]{2,1,0:T(8,128)(2,1)S(1)} %get-tuple-element.91), channel_id=1, source_target_pairs={{8,12},{9,13},{10,14},{11,15},{24,28},{25,29},{26,30},{27,31}} | collective-permute-start | bytes 983048 | tf_op jit(solution)/shard_map/ppermute | solution.py:74
  160.0 20.6 %collective-permute-start.59 = (bf16[2,64,1280]{2,1,0:T(8,128)(2,1)S(1)}, bf16[2,64,1280]{2,1,0:T(8,128)(2,1)S(1)}, u32[]{:S(2)}, u32[]{:S(2)}) collective-permute-start(bf16[2,64,1280]{2,1,0:T(8,128)(2,1)S(1)} %get-tuple-element.92), channel_id=1, source_target_pairs={{4,0},{5,1},{6,2},{7,3},{20,16},{21,17},{22,18},{23,19}} | collective-permute-start | bytes 983048 | tf_op jit(solution)/shard_map/ppermute | solution.py:74
  187.6 14.3 %collective-permute-start.46 = (bf16[2,16,2048]{2,1,0:T(8,128)(2,1)S(1)}, bf16[2,16,2048]{2,1,0:T(8,128)(2,1)S(1)}, u32[]{:S(2)}, u32[]{:S(2)}) collective-permute-start(bf16[2,16,2048]{2,1,0:T(8,128)(2,1)S(1)} %get-tuple-element.119), channel_id=1, source_target_pairs={{0,8},{4,12},{8,0},{12,4},{1,9},{5,13},{9,1},{13,5},{2,10},{6,14},... | collective-permute-start | bytes 393224 | tf_op jit(solution)/shard_map/ppermute | solution.py:34
  192.7 15.0 %collective-permute-start.54 = (bf16[1,16,2048]{2,1,0:T(8,128)(2,1)S(1)}, bf16[1,16,2048]{2,1,0:T(8,128)(2,1)S(1)}, u32[]{:S(2)}, u32[]{:S(2)}) collective-permute-start(bf16[1,16,2048]{2,1,0:T(8,128)(2,1)S(1)} %get-tuple-element.127), channel_id=1, source_target_pairs={{0,4},{4,0},{8,12},{12,8},{1,5},{5,1},{9,13},{13,9},{2,6},{6,2},{1... | collective-permute-start | bytes 196616 | tf_op jit(solution)/shard_map/ppermute | solution.py:34
  192.7 15.7 %collective-permute-start.55 = (bf16[1,16,2048]{2,1,0:T(8,128)(2,1)S(1)}, bf16[1,16,2048]{2,1,0:T(8,128)(2,1)S(1)}, u32[]{:S(2)}, u32[]{:S(2)}) collective-permute-start(bf16[1,16,2048]{2,1,0:T(8,128)(2,1)S(1)} %get-tuple-element.128), channel_id=1, source_target_pairs={{0,8},{4,12},{8,0},{12,4},{1,9},{5,13},{9,1},{13,5},{2,10},{6,14},... | collective-permute-start | bytes 196616 | tf_op jit(solution)/shard_map/ppermute | solution.py:34
  (58 other events, 598.3 us)
where the time goes:
time: 230 us; the launch traced here: 228 us
  starting transfers between devices  93.1 us (40%)
  waiting for transfers between devices  72 us (31%)
  Pallas kernels  43.8 us (19%)
  other arithmetic  7.92 us (3%)
  local copies, waits for them, and re-layouts  7.67 us (3%)
    ppermute x44, waiting for transfers between devices, swap(): return lax.ppermute(x, axis, [(a, a ^ k) for a in range(n)])  53.2 us
    ppermute x24, starting transfers between devices, line_sums(): came[s][w].append(lax.ppermute(value, axis, pairs))  49.7 us
    ppermute x44, starting transfers between devices, swap(): return lax.ppermute(x, axis, [(a, a ^ k) for a in range(n)])  43.4 us
    ppermute x24, waiting for transfers between devices, line_sums(): came[s][w].append(lax.ppermute(value, axis, pairs))  18.7 us
    pallas_call x4, Pallas kernels, second(): pl.pallas_call(functools.partial(second_kernel, count), out_shape=[out, o...  17.2 us
    pallas_call x1, Pallas kernels, attend(): pl.pallas_call(attend_kernel, out_shape=[bf16(rows // parts, cols)] * par...  14.2 us
    pallas_call x2, Pallas kernels, first(): pl.pallas_call(functools.partial(first_kernel, len(groups), batches, imag...  7.36 us
    pallas_call x1, Pallas kernels, project(): pl.pallas_call(functools.partial(project_kernel, count, splits), out_shap...  5.05 us
  transfers between devices with their start and end apart: 68, of which 25 were waited for; matrix products, arithmetic and copies ran while one was open for 4% of the time, Pallas kernels for 17%

commit v1 on v0

--- a/solution.py
+++ b/solution.py
@@ -59,16 +59,26 @@
     steps = ((lambda a: (a, a + 1)), (lambda a: (n - 1 - a, n - 2 - a)))
     sent = [[[] for _ in steps] for _ in streams]
     came = [[[] for _ in steps] for _ in streams]
-    results, waits = [], {}
+    results, waits, ready = [], {}, []
+
+    def drain(step):
+        while ready:
+            done, sums = ready.pop()
+            waits[step], result = finish(done, sums, [values[-1] for values in sent[0]], results)
+            results.append(result)
+
     for step in range(n + blocks - 1):
         for s, terms in enumerate(streams):
+            if s:
+                drain(step)
             for w, step_to in enumerate(steps):
                 value = terms[w][step % blocks]
                 if step:
-                    value = add16(value, came[s][w][-1])
+                    last = came[s][w][-1]
+                    if s and step in waits:
+                        last, _ = lax.optimization_barrier((last, waits[step]))
+                    value = add16(value, last)
                 sent[s][w].append(value)
-                if s and step in waits:
-                    value, _ = lax.optimization_barrier((value, waits[step]))
                 pairs = [step_to(a) for a in range(n - 1) if 0 <= step - a < blocks]
                 if pairs:
                     came[s][w].append(lax.ppermute(value, axis, pairs))
@@ -82,9 +92,8 @@
                     below = jnp.where(here == place, up[done + place], below)
                     above = jnp.where(here == place, down[done + n - 2 - place], above)
                 sums.append(below.astype(jnp.float32) + above.astype(jnp.float32))
-            after = came[0][0][done + n - 1] if done + n - 1 < len(came[0][0]) else None
-            waits[done + n], result = finish(done, sums, after, results)
-            results.append(result)
+            ready.append((done, sums))
+    drain(n + blocks - 1)
     return results
 
 
@@ -298,7 +307,7 @@
             down_ref[(batch + line - 1 - here) % batches, g] = part
 
 
-def first(groups, batches, w):
+def first(groups, batches, w, own):
     count = len(groups[0])
     blocks = [block for group in groups for block in group]
     rows, depth = blocks[0].shape
@@ -307,7 +316,7 @@
     return pl.pallas_call(
         functools.partial(first_kernel, len(groups), batches, images),
         out_shape=[out, out],
-        in_specs=[vmem()] + [anywhere()] * len(blocks),
+        in_specs=[vmem(), own] + [anywhere()] * (len(blocks) - 1),
         out_specs=[vmem(), vmem()],
         scratch_shapes=[
             bf16_scratch(rows * len(blocks), depth),
@@ -362,6 +371,42 @@
             transcendentals=rows * count * width,
         ),
     )(bias, goes, w, *totals)
+
+
+def place_kernel(count, hit_ref, bias_ref, text_ref, *rest):
+    blocks, out_ref, (cat_ref, sems) = rest[:count], rest[count], rest[-2:]
+    loads, low = [], 0
+    for k, block in enumerate(blocks):
+        place = cat_ref.at[low : low + block.shape[0]]
+        loads.append(pltpu.make_async_copy(block, place, sems.at[k]))
+        loads[-1].start()
+        low += block.shape[0]
+    hit = hit_ref[...]
+    covered = jnp.sum(hit.astype(jnp.float32), axis=1, keepdims=True) > 0
+    for load in loads:
+        load.wait()
+    placed = dot32(hit, cat_ref[...]) + bias_ref[...].reshape(1, -1)
+    out_ref[...] = jnp.where(covered, placed.astype(jnp.bfloat16), text_ref[...])
+
+
+def place_rows(blocks, hit, bias, text):
+    count = len(blocks)
+    return pl.pallas_call(
+        functools.partial(place_kernel, count),
+        out_shape=bf16(*text.shape),
+        in_specs=[vmem()] * 3 + [anywhere()] * count,
+        out_specs=vmem(),
+        scratch_shapes=[
+            bf16_scratch(hit.shape[1], text.shape[1]),
+            pltpu.SemaphoreType.DMA((count,)),
+        ],
+        compiler_params=pltpu.CompilerParams(vmem_limit_bytes=VMEM_BYTES // 2),
+        cost_estimate=pl.CostEstimate(
+            flops=2 * hit.shape[0] * hit.shape[1] * text.shape[1],
+            bytes_accessed=4 * text.shape[0] * text.shape[1],
+            transcendentals=0,
+        ),
+    )(hit, bias, text, *blocks)
 
 
 def local(
@@ -424,9 +469,9 @@
         rows_out = jnp.arange(seq_rows, dtype=jnp.int32)[:, None]
         return goes, (rows_out == slot_rows).astype(jnp.bfloat16)
 
-    blocks, proj_high = lax.optimization_barrier((list(blocks), proj_high))
-    goes, hit = places(blocks[0])
     blocks = [swap(block, "tensor", k) if k else block for k, block in enumerate(blocks)]
+    blocks[1], proj_high = lax.optimization_barrier((blocks[1], proj_high))
+    goes, hit = places(proj_high[tensors // 2])
     proj_blocks = {}
     for k, high in proj_high.items():
         for j, block in enumerate(gather_low(high, "tensor", tensors // 2)):
@@ -450,7 +495,8 @@
         high = swap(block, "tensor", tensors // 2)
         for k, line in enumerate(gather_low(high, "tensor", tensors // 2)):
             far[k].append(line)
-    streams = [first(near, batches, w_first), first(far, batches, w_first)]
+    near[0][1], _ = lax.optimization_barrier((near[0][1], far[0][:2]))
+    streams = [first(near, batches, w_first, hbm()), first(far, batches, w_first, anywhere())]
 
     columns = w_second.shape[1]
     shares = dps // tensors
@@ -463,18 +509,22 @@
             blocks.append(swap(moved, "dp", j) if j else moved)
         return blocks
 
-    arrived = []
+    arrived, pair_sums = [], []
 
     def finish(batch, sums, after, results):
+        if batch == batches - 2:
+            after = [after, results[-1]]
         if batch == batches - 1:
             arrived.append(to_shards(results[: batches - 2]))
-            after = arrived[0][1]
-        if after is not None:
-            sums, _ = lax.optimization_barrier((sums, after))
+            after = arrived[0][1:3]
+        sums, _ = lax.optimization_barrier((sums, (after, pair_sums[-1:])))
         rows_in = [part.reshape(-1, w_second.shape[0]) for part in sums]
         send, block = second(rows_in, b_first, goes[batch], w_second)
+        if batch == batches - 1:
+            send, results[-1] = lax.optimization_barrier((send, results[-1]))
         wait = send
         block = add16(block, swap(send, "tensor", 1))
+        pair_sums.append(block)
         step = 2
         while step < tensors:
             half = block.shape[0] // 2
@@ -483,24 +533,23 @@
         return wait, block.reshape(dps, part * images, columns)
 
     held = line_sums(streams, "dp", finish)
-    for block in held[batches - 2 :]:
-        arrived.append(to_shards([block]))
-    arrived = jnp.concatenate([jnp.stack(blocks) for blocks in arrived], axis=1)
-    arrived = arrived.reshape(tensors, shares, -1, columns)
-    visual = []
-    for k in range(tensors):
-        moved = pick(arrived, (tensor_at ^ k) ^ (dp_at // shares))
-        moved = swap(moved, "tensor", k) if k else moved
-        if shares > 1:
-            moved = jnp.concatenate(
-                [pick(moved, (dp_at % shares) ^ j) for j in range(shares)], axis=-1
-            )
-        visual.append(moved.reshape(-1, shares * columns))
-    visual = jnp.concatenate(visual, axis=0)
-
-    covered = jnp.sum(hit, axis=1, keepdims=True, dtype=jnp.float32) > 0
-    placed = dot32(hit, visual) + b_second
-    return jnp.where(covered, placed.astype(jnp.bfloat16), text_embed)
+    arrived.append(to_shards(held[batches - 2 :]))
+    visual = [[] for _ in range(tensors)]
+    for group in (arrived[:-1], arrived[-1:]):
+        group = jnp.concatenate([jnp.stack(blocks) for blocks in group], axis=1)
+        group = group.reshape(tensors, shares, -1, columns)
+        for k in range(tensors):
+            moved = pick(group, (tensor_at ^ k) ^ (dp_at // shares))
+            moved = swap(moved, "tensor", k) if k else moved
+            if shares > 1:
+                moved = jnp.concatenate(
+                    [pick(moved, (dp_at % shares) ^ j) for j in range(shares)], axis=-1
+                )
+            visual[k].append(moved.reshape(-1, shares * columns))
+    visual = [block for blocks in visual for block in blocks]
+    if any(block.shape[0] % 16 for block in visual):
+        visual = [jnp.concatenate(visual, axis=0)]
+    return place_rows(visual, hit, b_second, text_embed)
 
 
 def solution(mesh):

time: 230 us -> 221 us (0.961)
  starting transfers between devices: 93.1 us -> 82 us
  waiting for transfers between devices: 72 us -> 76.2 us
  Pallas kernels: 43.8 us -> 46.5 us
    ppermute x44, starting transfers between devices: 43.4 us -> 33.8 us  [swap(): return lax.ppermute(x, axis, [(a, a ^ k) for a in range(n)])]
    ppermute x24, waiting for transfers between devices: 18.7 us -> 25.6 us  [line_sums(): came[s][w].append(lax.ppermute(value, axis, pairs))]
    pallas_call x0 -> x1, Pallas kernels: none -> 3.29 us  [place_rows(): pl.pallas_call(functools.partial(place_kernel, count), out_shape=bf16(*te...]
    ppermute x44, waiting for transfers between devices: 53.2 us -> 50.6 us  [swap(): return lax.ppermute(x, axis, [(a, a ^ k) for a in range(n)])]
  transfers between devices with their start and end apart: 68 -> 68, of which waited for: 25 -> 29; matrix products, arithmetic and copies ran while one was open for 4% -> 4% of each run, Pallas kernels for 17% -> 17%
where the time goes in v1:
time: 221 us
  starting transfers between devices  82 us (37%)
  waiting for transfers between devices  76.2 us (34%)
  Pallas kernels  46.5 us (21%)
  local copies, waits for them, and re-layouts  7.72 us (3%)
  other arithmetic  5.67 us (3%)
  between operations  2.46 us (1%)
    ppermute x44, waiting for transfers between devices, swap(): return lax.ppermute(x, axis, [(a, a ^ k) for a in range(n)])  50.6 us
    ppermute x24, starting transfers between devices, line_sums(): came[s][w].append(lax.ppermute(value, axis, pairs))  48.2 us
    ppermute x44, starting transfers between devices, swap(): return lax.ppermute(x, axis, [(a, a ^ k) for a in range(n)])  33.8 us
    ppermute x24, waiting for transfers between devices, line_sums(): came[s][w].append(lax.ppermute(value, axis, pairs))  25.6 us
    pallas_call x4, Pallas kernels, second(): pl.pallas_call(functools.partial(second_kernel, count), out_shape=[out, o...  17.2 us
    pallas_call x1, Pallas kernels, attend(): pl.pallas_call(attend_kernel, out_shape=[bf16(rows // parts, cols)] * par...  14.1 us
    pallas_call x2, Pallas kernels, first(): pl.pallas_call(functools.partial(first_kernel, len(groups), batches, imag...  7.12 us
    pallas_call x1, Pallas kernels, project(): pl.pallas_call(functools.partial(project_kernel, count, splits), out_shap...  4.75 us
  transfers between devices with their start and end apart: 68, of which 29 were waited for; matrix products, arithmetic and copies ran while one was open for 4% of the time, Pallas kernels for 17%

profile of v1, /device:TPU:0, one launch (start us, length us, event | category | flops | bytes accessed | tf_op | source)
XLA Modules:
  0.0 220.5 jit_solution(8605805367539199327)
XLA Ops:
  3.0 14.1 %shard_map.136 = (bf16[256,320]{1,0:T(8,128)(2,1)}, bf16[256,320]{1,0:T(8,128)(2,1)}, bf16[256,320]{1,0:T(8,128)(2,1)}, bf16[256,320]{1,0:T(8,128)(2,1)}) custom-call(s32[1,2]{1,0:T(1,128)} %grid_ref.1, bf16[1024,1280]{1,0:T(8,128)(2,1)} %x_hbm.3, f32[1280]{0:T(1024)} %gain_ref.2, bf16[3,320,1280]{2,1,0:T(8,128)(2,1)} %bitcast.184, f32[3,320]{1,0:T(4,128)} %b_ref.1), custom_call_target="tpu_custom_call" | custom-call | flops 3858759680 | bytes 7700480 | tf_op jit(solution)/shard_map/pallas_call | solution.py:199
  30.8 3.5 %collective-permute-done.4 = s32[256]{0:T(256)S(1)} collective-permute-done((s32[256]{0:T(256)S(1)}, s32[256]{0:T(256)S(1)}, u32[]{:S(2)}, u32[]{:S(2)}) %collective-permute-start.4) | collective-permute-done | bytes 1056 | tf_op jit(solution)/shard_map/ppermute | solution.py:34
  39.3 4.7 %shard_map.137 = (bf16[64,1280]{1,0:T(8,128)(2,1)}, bf16[64,1280]{1,0:T(8,128)(2,1)}, bf16[64,1280]{1,0:T(8,128)(2,1)}, bf16[64,1280]{1,0:T(8,128)(2,1)}) custom-call(bf16[1024,1280]{1,0:T(8,128)(2,1)} %x_hbm.3, f32[1280]{0:T(1024)S(1)} %copy-done.6, f32[1280]{0:T(1024)S(1)} %copy-done.7, bf16[256,320]{1,0:T(8,128)(2,1)S(1)} %copy-done.2, ...), custom_call_target="tpu_custom_call" | custom-call | flops 838860800 | bytes 5242880 | tf_op jit(solution)/shard_map/pallas_call | solution.py:261
  46.4 3.6 %collective-permute-start.13 = (bf16[64,1280]{1,0:T(8,128)(2,1)}, bf16[64,1280]{1,0:T(8,128)(2,1)S(1)}, u32[]{:S(2)}, u32[]{:S(2)}) collective-permute-start(bf16[64,1280]{1,0:T(8,128)(2,1)} %get-tuple-element.71), channel_id=1, source_target_pairs={{0,12},{4,8},{8,4},{12,0},{1,13},{5,9},{9,5},{13,1},{2,14},{6,10},... | collective-permute-start | bytes 491528 | tf_op jit(solution)/shard_map/ppermute | solution.py:34
  51.2 8.0 %collective-permute-done.12.rest_2_ = bf16[64,1280]{1,0:T(8,128)(2,1)S(1)} collective-permute-done((bf16[64,1280]{1,0:T(8,128)(2,1)}, bf16[64,1280]{1,0:T(8,128)(2,1)S(1)}, u32[]{:S(2)}, u32[]{:S(2)}) %collective-permute-start.12) | collective-permute-done | bytes 163872 | tf_op jit(solution)/shard_map/ppermute | solution.py:34
  67.3 3.7 %collective-permute-start.18 = (bf16[2,64,1280]{2,1,0:T(8,128)(2,1)S(1)}, bf16[2,64,1280]{2,1,0:T(8,128)(2,1)S(1)}, u32[]{:S(2)}, u32[]{:S(2)}) collective-permute-start(bf16[2,64,1280]{2,1,0:T(8,128)(2,1)S(1)} %slice_bitcast_fusion.3), channel_id=1, source_target_pairs={{0,4},{1,5},{2,6},{3,7},{16,20},{17,21},{18,22},{19,23}} | collective-permute-start | bytes 983048 | tf_op jit(solution)/shard_map/ppermute | solution.py:84
  73.0 3.7 %shard_map.139 = (bf16[4,2,64,1280]{3,2,1,0:T(8,128)(2,1)S(1)}, bf16[4,2,64,1280]{3,2,1,0:T(8,128)(2,1)S(1)}) custom-call(bf16[1280,1280]{1,0:T(8,128)(2,1)S(1)} %copy-done.10, bf16[64,1280]{1,0:T(8,128)(2,1)S(1)} %collective-permute-done.10.rest_0_, bf16[64,1280]{1,0:T(8,128)(2,1)S(1)} %collective-permute-done.11.rest_1_, ...), custom_call_target="tpu_custom_call" | custom-call | flops 1677721600 | bytes 7208960 | tf_op jit(solution)/shard_map/pallas_call | solution.py:316
  79.6 3.5 %collective-permute-start.19 = (bf16[2,64,1280]{2,1,0:T(8,128)(2,1)S(1)}, bf16[2,64,1280]{2,1,0:T(8,128)(2,1)S(1)}, u32[]{:S(2)}, u32[]{:S(2)}) collective-permute-start(bf16[2,64,1280]{2,1,0:T(8,128)(2,1)S(1)} %fusion), channel_id=1, source_target_pairs={{0,4},{4,8},{1,5},{5,9},{2,6},{6,10},{3,7},{7,11},{16,20},{20,24},... | collective-permute-start | bytes 983048 | tf_op jit(solution)/shard_map/ppermute | solution.py:84
  86.9 4.4 %collective-permute-start.31 = (bf16[2,64,1280]{2,1,0:T(8,128)(2,1)S(1)}, bf16[2,64,1280]{2,1,0:T(8,128)(2,1)S(1)}, u32[]{:S(2)}, u32[]{:S(2)}) collective-permute-start(bf16[2,64,1280]{2,1,0:T(8,128)(2,1)S(1)} %fusion.6), channel_id=1, source_target_pairs={{0,4},{4,8},{1,5},{5,9},{2,6},{6,10},{3,7},{7,11},{16,20},{20,24},... | collective-permute-start | bytes 983048 | tf_op jit(solution)/shard_map/ppermute | solution.py:84
  93.9 4.4 %collective-permute-start.20 = (bf16[2,64,1280]{2,1,0:T(8,128)(2,1)S(1)}, bf16[2,64,1280]{2,1,0:T(8,128)(2,1)S(1)}, u32[]{:S(2)}, u32[]{:S(2)}) collective-permute-start(bf16[2,64,1280]{2,1,0:T(8,128)(2,1)S(1)} %fusion.4), channel_id=1, source_target_pairs={{0,4},{4,8},{8,12},{1,5},{5,9},{9,13},{2,6},{6,10},{10,14},{3,7},{... | collective-permute-start | bytes 983048 | tf_op jit(solution)/shard_map/ppermute | solution.py:84
  101.0 4.4 %collective-permute-start.32 = (bf16[2,64,1280]{2,1,0:T(8,128)(2,1)S(1)}, bf16[2,64,1280]{2,1,0:T(8,128)(2,1)S(1)}, u32[]{:S(2)}, u32[]{:S(2)}) collective-permute-start(bf16[2,64,1280]{2,1,0:T(8,128)(2,1)S(1)} %fusion.8), channel_id=1, source_target_pairs={{0,4},{4,8},{8,12},{1,5},{5,9},{9,13},{2,6},{6,10},{10,14},{3,7},{... | collective-permute-start | bytes 983048 | tf_op jit(solution)/shard_map/ppermute | solution.py:84
  108.6 4.1 %collective-permute-start.36 = (bf16[2,64,1280]{2,1,0:T(8,128)(2,1)S(1)}, bf16[2,64,1280]{2,1,0:T(8,128)(2,1)S(1)}, u32[]{:S(2)}, u32[]{:S(2)}) collective-permute-start(bf16[2,64,1280]{2,1,0:T(8,128)(2,1)S(1)} %get-tuple-element.112), channel_id=1, source_target_pairs={{0,4},{4,8},{8,12},{1,5},{5,9},{9,13},{2,6},{6,10},{10,14},{3,7},{... | collective-permute-start | bytes 983048 | tf_op jit(solution)/shard_map/ppermute | solution.py:84
  115.6 5.3 %collective-permute-start.40 = (bf16[2,64,1280]{2,1,0:T(8,128)(2,1)S(1)}, bf16[2,64,1280]{2,1,0:T(8,128)(2,1)S(1)}, u32[]{:S(2)}, u32[]{:S(2)}) collective-permute-start(bf16[2,64,1280]{2,1,0:T(8,128)(2,1)S(1)} %get-tuple-element.110), channel_id=1, source_target_pairs={{0,4},{4,8},{8,12},{1,5},{5,9},{9,13},{2,6},{6,10},{10,14},{3,7},{... | collective-permute-start | bytes 983048 | tf_op jit(solution)/shard_map/ppermute | solution.py:84
  128.1 4.3 %shard_map.140 = (bf16[128,2048]{1,0:T(8,128)(2,1)S(1)}, bf16[128,2048]{1,0:T(8,128)(2,1)S(1)}) custom-call(f32[1280]{0:T(1024)S(1)} %copy-done.5, s32[1,256]{1,0:T(1,128)S(1)} %get-tuple-element.140.goes_ref, bf16[1280,2048]{1,0:T(8,128)(2,1)} %w_hbm.7, f32[128,1280]{1,0:T(8,128)S(1)} %bitcast.154, f32[128,1280]{1,0:T(8,128)S(1)} %bitcast.155), custom_call_target="tpu_custom_call" | custom-call | flops 1342177280 | bytes 5242880 | tf_op jit(solution)/shard_map/pallas_call | solution.py:357
  135.7 3.8 %collective-permute-done.43 = bf16[2,64,1280]{2,1,0:T(8,128)(2,1)S(1)} collective-permute-done((bf16[2,64,1280]{2,1,0:T(8,128)(2,1)S(1)}, bf16[2,64,1280]{2,1,0:T(8,128)(2,1)S(1)}, u32[]{:S(2)}, u32[]{:S(2)}) %collective-permute-start.43) | collective-permute-done | bytes 327712 | tf_op jit(solution)/shard_map/ppermute | solution.py:84
  142.0 4.3 %shard_map.141 = (bf16[128,2048]{1,0:T(8,128)(2,1)S(1)}, bf16[128,2048]{1,0:T(8,128)(2,1)S(1)}) custom-call(f32[1280]{0:T(1024)S(1)} %copy-done.5, s32[1,256]{1,0:T(1,128)S(1)} %get-tuple-element.139.goes_ref, bf16[1280,2048]{1,0:T(8,128)(2,1)} %w_hbm.7, f32[128,1280]{1,0:T(8,128)S(1)} %bitcast.153, f32[128,1280]{1,0:T(8,128)S(1)} %bitcast.158), custom_call_target="tpu_custom_call" | custom-call | flops 1342177280 | bytes 5242880 | tf_op jit(solution)/shard_map/pallas_call | solution.py:357
  146.4 5.6 %collective-permute-done.53 = bf16[2,64,1280]{2,1,0:T(8,128)(2,1)S(1)} collective-permute-done((bf16[2,64,1280]{2,1,0:T(8,128)(2,1)S(1)}, bf16[2,64,1280]{2,1,0:T(8,128)(2,1)S(1)}, u32[]{:S(2)}, u32[]{:S(2)}) %collective-permute-start.53) | collective-permute-done | bytes 327712 | tf_op jit(solution)/shard_map/ppermute | solution.py:84
  155.2 3.8 %collective-permute-done.50 = bf16[2,64,1280]{2,1,0:T(8,128)(2,1)S(1)} collective-permute-done((bf16[2,64,1280]{2,1,0:T(8,128)(2,1)S(1)}, bf16[2,64,1280]{2,1,0:T(8,128)(2,1)S(1)}, u32[]{:S(2)}, u32[]{:S(2)}) %collective-permute-start.50) | collective-permute-done | bytes 327712 | tf_op jit(solution)/shard_map/ppermute | solution.py:84
  163.1 4.3 %shard_map.142 = (bf16[128,2048]{1,0:T(8,128)(2,1)S(1)}, bf16[128,2048]{1,0:T(8,128)(2,1)S(1)}) custom-call(f32[1280]{0:T(1024)S(1)} %copy-done.5, s32[1,256]{1,0:T(1,128)S(1)} %get-tuple-element.137.goes_ref, bf16[1280,2048]{1,0:T(8,128)(2,1)} %w_hbm.7, f32[128,1280]{1,0:T(8,128)S(1)} %bitcast.152, f32[128,1280]{1,0:T(8,128)S(1)} %bitcast.157), custom_call_target="tpu_custom_call" | custom-call | flops 1342177280 | bytes 5242880 | tf_op jit(solution)/shard_map/pallas_call | solution.py:357
  176.6 4.1 %collective-permute-done.47 = bf16[2,16,2048]{2,1,0:T(8,128)(2,1)S(1)} collective-permute-done((bf16[2,16,2048]{2,1,0:T(8,128)(2,1)S(1)}, bf16[2,16,2048]{2,1,0:T(8,128)(2,1)S(1)}, u32[]{:S(2)}, u32[]{:S(2)}) %collective-permute-start.47) | collective-permute-done | bytes 131104 | tf_op jit(solution)/shard_map/ppermute | solution.py:34
  180.7 4.3 %shard_map.143 = (bf16[128,2048]{1,0:T(8,128)(2,1)S(1)}, bf16[128,2048]{1,0:T(8,128)(2,1)S(1)}) custom-call(f32[1280]{0:T(1024)S(1)} %copy-done.5, s32[1,256]{1,0:T(1,128)S(1)} %get-tuple-element.138.goes_ref, bf16[1280,2048]{1,0:T(8,128)(2,1)} %w_hbm.7, f32[128,1280]{1,0:T(8,128)S(1)} %bitcast.151, f32[128,1280]{1,0:T(8,128)S(1)} %bitcast.156), custom_call_target="tpu_custom_call" | custom-call | flops 1342177280 | bytes 5242880 | tf_op jit(solution)/shard_map/pallas_call | solution.py:357
  187.7 5.2 %collective-permute-done.48 = bf16[2,16,2048]{2,1,0:T(8,128)(2,1)S(1)} collective-permute-done((bf16[2,16,2048]{2,1,0:T(8,128)(2,1)S(1)}, bf16[2,16,2048]{2,1,0:T(8,128)(2,1)S(1)}, u32[]{:S(2)}, u32[]{:S(2)}) %collective-permute-start.48) | collective-permute-done | bytes 131104 | tf_op jit(solution)/shard_map/ppermute | solution.py:34
  202.3 6.2 %collective-permute-done.60 = bf16[2,16,2048]{2,1,0:T(8,128)(2,1)S(1)} collective-permute-done((bf16[2,16,2048]{2,1,0:T(8,128)(2,1)S(1)}, bf16[2,16,2048]{2,1,0:T(8,128)(2,1)S(1)}, u32[]{:S(2)}, u32[]{:S(2)}) %collective-permute-start.60) | collective-permute-done | bytes 131104 | tf_op jit(solution)/shard_map/ppermute | solution.py:34
  210.6 4.5 %collective-permute-done.65 = bf16[1,32,2048]{2,1,0:T(8,128)(2,1)S(1)} collective-permute-done((bf16[1,32,2048]{2,1,0:T(8,128)(2,1)S(1)}, bf16[1,32,2048]{2,1,0:T(8,128)(2,1)S(1)}, u32[]{:S(2)}, u32[]{:S(2)}) %collective-permute-start.65) | collective-permute-done | bytes 131104 | tf_op jit(solution)/shard_map/ppermute | solution.py:34
  (215 shorter events, 100.1 us)
Async XLA Ops:
  0.0 22.2 %collective-permute-start.1 = (bf16[320,1280]{1,0:T(8,128)(2,1)}, bf16[320,1280]{1,0:T(8,128)(2,1)S(1)}, u32[]{:S(2)}, u32[]{:S(2)}) collective-permute-start(bf16[320,1280]{1,0:T(8,128)(2,1)} %rest_4_), channel_id=1, source_target_pairs={{0,2},{1,3},{2,0},{3,1},{4,6},{5,7},{6,4},{7,5},{8,10},{9,11},{10,... | collective-permute-start | bytes 2457608 | tf_op jit(solution)/shard_map/ppermute | solution.py:34
  17.2 20.2 %collective-permute-start.5 = (bf16[256,320]{1,0:T(8,128)(2,1)}, bf16[256,320]{1,0:T(8,128)(2,1)}, u32[]{:S(2)}, u32[]{:S(2)}) collective-permute-start(bf16[256,320]{1,0:T(8,128)(2,1)} %get-tuple-element.64), channel_id=1, source_target_pairs={{0,2},{1,3},{2,0},{3,1},{4,6},{5,7},{6,4},{7,5},{8,10},{9,11},{10,... | collective-permute-start | bytes 491528 | tf_op jit(solution)/shard_map/ppermute | solution.py:34
  17.3 20.1 %collective-permute-start.6 = (bf16[256,320]{1,0:T(8,128)(2,1)}, bf16[256,320]{1,0:T(8,128)(2,1)}, u32[]{:S(2)}, u32[]{:S(2)}) collective-permute-start(bf16[256,320]{1,0:T(8,128)(2,1)} %get-tuple-element.65), channel_id=1, source_target_pairs={{0,3},{1,2},{2,1},{3,0},{4,7},{5,6},{6,5},{7,4},{8,11},{9,10},{10,... | collective-permute-start | bytes 491528 | tf_op jit(solution)/shard_map/ppermute | solution.py:34
  45.7 13.5 %collective-permute-start.12 = (bf16[64,1280]{1,0:T(8,128)(2,1)}, bf16[64,1280]{1,0:T(8,128)(2,1)S(1)}, u32[]{:S(2)}, u32[]{:S(2)}) collective-permute-start(bf16[64,1280]{1,0:T(8,128)(2,1)} %get-tuple-element.70), channel_id=1, source_target_pairs={{0,8},{4,12},{8,0},{12,4},{1,9},{5,13},{9,1},{13,5},{2,10},{6,14},... | collective-permute-start | bytes 491528 | tf_op jit(solution)/shard_map/ppermute | solution.py:34
  46.4 12.8 %collective-permute-start.13 = (bf16[64,1280]{1,0:T(8,128)(2,1)}, bf16[64,1280]{1,0:T(8,128)(2,1)S(1)}, u32[]{:S(2)}, u32[]{:S(2)}) collective-permute-start(bf16[64,1280]{1,0:T(8,128)(2,1)} %get-tuple-element.71), channel_id=1, source_target_pairs={{0,12},{4,8},{8,4},{12,0},{1,13},{5,9},{9,5},{13,1},{2,14},{6,10},... | collective-permute-start | bytes 491528 | tf_op jit(solution)/shard_map/ppermute | solution.py:34
  78.8 12.5 %collective-permute-start.33 = (bf16[2,64,1280]{2,1,0:T(8,128)(2,1)S(1)}, bf16[2,64,1280]{2,1,0:T(8,128)(2,1)S(1)}, u32[]{:S(2)}, u32[]{:S(2)}) collective-permute-start(bf16[2,64,1280]{2,1,0:T(8,128)(2,1)S(1)} %slice_bitcast_fusion), channel_id=1, source_target_pairs={{12,8},{13,9},{14,10},{15,11},{28,24},{29,25},{30,26},{31,27}} | collective-permute-start | bytes 983048 | tf_op jit(solution)/shard_map/ppermute | solution.py:84
  79.6 14.2 %collective-permute-start.19 = (bf16[2,64,1280]{2,1,0:T(8,128)(2,1)S(1)}, bf16[2,64,1280]{2,1,0:T(8,128)(2,1)S(1)}, u32[]{:S(2)}, u32[]{:S(2)}) collective-permute-start(bf16[2,64,1280]{2,1,0:T(8,128)(2,1)S(1)} %fusion), channel_id=1, source_target_pairs={{0,4},{4,8},{1,5},{5,9},{2,6},{6,10},{3,7},{7,11},{16,20},{20,24},... | collective-permute-start | bytes 983048 | tf_op jit(solution)/shard_map/ppermute | solution.py:84
  83.2 15.1 %collective-permute-start.22 = (bf16[2,64,1280]{2,1,0:T(8,128)(2,1)S(1)}, bf16[2,64,1280]{2,1,0:T(8,128)(2,1)S(1)}, u32[]{:S(2)}, u32[]{:S(2)}) collective-permute-start(bf16[2,64,1280]{2,1,0:T(8,128)(2,1)S(1)} %fusion.2), channel_id=1, source_target_pairs={{12,8},{8,4},{13,9},{9,5},{14,10},{10,6},{15,11},{11,7},{28,24},{2... | collective-permute-start | bytes 983048 | tf_op jit(solution)/shard_map/ppermute | solution.py:84
  86.9 14.0 %collective-permute-start.31 = (bf16[2,64,1280]{2,1,0:T(8,128)(2,1)S(1)}, bf16[2,64,1280]{2,1,0:T(8,128)(2,1)S(1)}, u32[]{:S(2)}, u32[]{:S(2)}) collective-permute-start(bf16[2,64,1280]{2,1,0:T(8,128)(2,1)S(1)} %fusion.6), channel_id=1, source_target_pairs={{0,4},{4,8},{1,5},{5,9},{2,6},{6,10},{3,7},{7,11},{16,20},{20,24},... | collective-permute-start | bytes 983048 | tf_op jit(solution)/shard_map/ppermute | solution.py:84
  91.4 14.0 %collective-permute-start.34 = (bf16[2,64,1280]{2,1,0:T(8,128)(2,1)S(1)}, bf16[2,64,1280]{2,1,0:T(8,128)(2,1)S(1)}, u32[]{:S(2)}, u32[]{:S(2)}) collective-permute-start(bf16[2,64,1280]{2,1,0:T(8,128)(2,1)S(1)} %fusion.10), channel_id=1, source_target_pairs={{12,8},{8,4},{13,9},{9,5},{14,10},{10,6},{15,11},{11,7},{28,24},{2... | collective-permute-start | bytes 983048 | tf_op jit(solution)/shard_map/ppermute | solution.py:84
  93.9 14.0 %collective-permute-start.20 = (bf16[2,64,1280]{2,1,0:T(8,128)(2,1)S(1)}, bf16[2,64,1280]{2,1,0:T(8,128)(2,1)S(1)}, u32[]{:S(2)}, u32[]{:S(2)}) collective-permute-start(bf16[2,64,1280]{2,1,0:T(8,128)(2,1)S(1)} %fusion.4), channel_id=1, source_target_pairs={{0,4},{4,8},{8,12},{1,5},{5,9},{9,13},{2,6},{6,10},{10,14},{3,7},{... | collective-permute-start | bytes 983048 | tf_op jit(solution)/shard_map/ppermute | solution.py:84
  101.0 14.0 %collective-permute-start.32 = (bf16[2,64,1280]{2,1,0:T(8,128)(2,1)S(1)}, bf16[2,64,1280]{2,1,0:T(8,128)(2,1)S(1)}, u32[]{:S(2)}, u32[]{:S(2)}) collective-permute-start(bf16[2,64,1280]{2,1,0:T(8,128)(2,1)S(1)} %fusion.8), channel_id=1, source_target_pairs={{0,4},{4,8},{8,12},{1,5},{5,9},{9,13},{2,6},{6,10},{10,14},{3,7},{... | collective-permute-start | bytes 983048 | tf_op jit(solution)/shard_map/ppermute | solution.py:84
  108.6 13.6 %collective-permute-start.36 = (bf16[2,64,1280]{2,1,0:T(8,128)(2,1)S(1)}, bf16[2,64,1280]{2,1,0:T(8,128)(2,1)S(1)}, u32[]{:S(2)}, u32[]{:S(2)}) collective-permute-start(bf16[2,64,1280]{2,1,0:T(8,128)(2,1)S(1)} %get-tuple-element.112), channel_id=1, source_target_pairs={{0,4},{4,8},{8,12},{1,5},{5,9},{9,13},{2,6},{6,10},{10,14},{3,7},{... | collective-permute-start | bytes 983048 | tf_op jit(solution)/shard_map/ppermute | solution.py:84
  112.7 12.7 %collective-permute-start.37 = (bf16[2,64,1280]{2,1,0:T(8,128)(2,1)S(1)}, bf16[2,64,1280]{2,1,0:T(8,128)(2,1)S(1)}, u32[]{:S(2)}, u32[]{:S(2)}) collective-permute-start(bf16[2,64,1280]{2,1,0:T(8,128)(2,1)S(1)} %get-tuple-element.136), channel_id=1, source_target_pairs={{12,8},{8,4},{4,0},{13,9},{9,5},{5,1},{14,10},{10,6},{6,2},{15,11}... | collective-permute-start | bytes 983048 | tf_op jit(solution)/shard_map/ppermute | solution.py:84
  115.6 16.8 %collective-permute-start.40 = (bf16[2,64,1280]{2,1,0:T(8,128)(2,1)S(1)}, bf16[2,64,1280]{2,1,0:T(8,128)(2,1)S(1)}, u32[]{:S(2)}, u32[]{:S(2)}) collective-permute-start(bf16[2,64,1280]{2,1,0:T(8,128)(2,1)S(1)} %get-tuple-element.110), channel_id=1, source_target_pairs={{0,4},{4,8},{8,12},{1,5},{5,9},{9,13},{2,6},{6,10},{10,14},{3,7},{... | collective-permute-start | bytes 983048 | tf_op jit(solution)/shard_map/ppermute | solution.py:84
  126.5 13.0 %collective-permute-start.43 = (bf16[2,64,1280]{2,1,0:T(8,128)(2,1)S(1)}, bf16[2,64,1280]{2,1,0:T(8,128)(2,1)S(1)}, u32[]{:S(2)}, u32[]{:S(2)}) collective-permute-start(bf16[2,64,1280]{2,1,0:T(8,128)(2,1)S(1)} %get-tuple-element.135), channel_id=1, source_target_pairs={{8,4},{4,0},{9,5},{5,1},{10,6},{6,2},{11,7},{7,3},{24,20},{20,16},... | collective-permute-start | bytes 983048 | tf_op jit(solution)/shard_map/ppermute | solution.py:84
  133.6 12.9 %collective-permute-start.51 = (bf16[2,64,1280]{2,1,0:T(8,128)(2,1)S(1)}, bf16[2,64,1280]{2,1,0:T(8,128)(2,1)S(1)}, u32[]{:S(2)}, u32[]{:S(2)}) collective-permute-start(bf16[2,64,1280]{2,1,0:T(8,128)(2,1)S(1)} %get-tuple-element.106), channel_id=1, source_target_pairs={{4,8},{8,12},{5,9},{9,13},{6,10},{10,14},{7,11},{11,15},{20,24},{2... | collective-permute-start | bytes 983048 | tf_op jit(solution)/shard_map/ppermute | solution.py:84
  134.4 17.7 %collective-permute-start.53 = (bf16[2,64,1280]{2,1,0:T(8,128)(2,1)S(1)}, bf16[2,64,1280]{2,1,0:T(8,128)(2,1)S(1)}, u32[]{:S(2)}, u32[]{:S(2)}) collective-permute-start(bf16[2,64,1280]{2,1,0:T(8,128)(2,1)S(1)} %add_convert_fusion.4), channel_id=1, source_target_pairs={{8,4},{4,0},{9,5},{5,1},{10,6},{6,2},{11,7},{7,3},{24,20},{20,16},... | collective-permute-start | bytes 983048 | tf_op jit(solution)/shard_map/ppermute | solution.py:84
  139.9 14.8 %collective-permute-start.49 = (bf16[2,64,1280]{2,1,0:T(8,128)(2,1)S(1)}, bf16[2,64,1280]{2,1,0:T(8,128)(2,1)S(1)}, u32[]{:S(2)}, u32[]{:S(2)}) collective-permute-start(bf16[2,64,1280]{2,1,0:T(8,128)(2,1)S(1)} %get-tuple-element.102), channel_id=1, source_target_pairs={{8,12},{9,13},{10,14},{11,15},{24,28},{25,29},{26,30},{27,31}} | collective-permute-start | bytes 983048 | tf_op jit(solution)/shard_map/ppermute | solution.py:84
  140.6 18.5 %collective-permute-start.50 = (bf16[2,64,1280]{2,1,0:T(8,128)(2,1)S(1)}, bf16[2,64,1280]{2,1,0:T(8,128)(2,1)S(1)}, u32[]{:S(2)}, u32[]{:S(2)}) collective-permute-start(bf16[2,64,1280]{2,1,0:T(8,128)(2,1)S(1)} %get-tuple-element.133), channel_id=1, source_target_pairs={{4,0},{5,1},{6,2},{7,3},{20,16},{21,17},{22,18},{23,19}} | collective-permute-start | bytes 983048 | tf_op jit(solution)/shard_map/ppermute | solution.py:84
  146.4 13.0 %collective-permute-start.44 = (bf16[128,2048]{1,0:T(8,128)(2,1)S(1)}, bf16[128,2048]{1,0:T(8,128)(2,1)S(1)}, u32[]{:S(2)}, u32[]{:S(2)}) collective-permute-start(bf16[128,2048]{1,0:T(8,128)(2,1)S(1)} %get-tuple-element.84), channel_id=1, source_target_pairs={{0,1},{1,0},{2,3},{3,2},{4,5},{5,4},{6,7},{7,6},{8,9},{9,8},{10,11... | collective-permute-start | bytes 1572872 | tf_op jit(solution)/shard_map/ppermute | solution.py:34
  152.1 21.0 %collective-permute-start.54 = (bf16[2,64,1280]{2,1,0:T(8,128)(2,1)S(1)}, bf16[2,64,1280]{2,1,0:T(8,128)(2,1)S(1)}, u32[]{:S(2)}, u32[]{:S(2)}) collective-permute-start(bf16[2,64,1280]{2,1,0:T(8,128)(2,1)S(1)} %fusion.11), channel_id=1, source_target_pairs={{4,0},{5,1},{6,2},{7,3},{20,16},{21,17},{22,18},{23,19}} | collective-permute-start | bytes 983048 | tf_op jit(solution)/shard_map/ppermute | solution.py:84
  153.8 13.7 %collective-permute-start.52 = (bf16[2,64,1280]{2,1,0:T(8,128)(2,1)S(1)}, bf16[2,64,1280]{2,1,0:T(8,128)(2,1)S(1)}, u32[]{:S(2)}, u32[]{:S(2)}) collective-permute-start(bf16[2,64,1280]{2,1,0:T(8,128)(2,1)S(1)} %get-tuple-element.100), channel_id=1, source_target_pairs={{8,12},{9,13},{10,14},{11,15},{24,28},{25,29},{26,30},{27,31}} | collective-permute-start | bytes 983048 | tf_op jit(solution)/shard_map/ppermute | solution.py:84
  195.9 12.7 %collective-permute-start.60 = (bf16[2,16,2048]{2,1,0:T(8,128)(2,1)S(1)}, bf16[2,16,2048]{2,1,0:T(8,128)(2,1)S(1)}, u32[]{:S(2)}, u32[]{:S(2)}) collective-permute-start(bf16[2,16,2048]{2,1,0:T(8,128)(2,1)S(1)} %get-tuple-element.127), channel_id=1, source_target_pairs={{0,8},{4,12},{8,0},{12,4},{1,9},{5,13},{9,1},{13,5},{2,10},{6,14},... | collective-permute-start | bytes 393224 | tf_op jit(solution)/shard_map/ppermute | solution.py:34
  (57 other events, 524.5 us)

commit v2 on v1

--- a/solution.py
+++ b/solution.py
@@ -64,7 +64,8 @@
     def drain(step):
         while ready:
             done, sums = ready.pop()
-            waits[step], result = finish(done, sums, [values[-1] for values in sent[0]], results)
+            after = [values[-1] for ways in sent for values in ways]
+            waits[step], result = finish(done, sums, after, results, came[-1])
             results.append(result)
 
     for step in range(n + blocks - 1):
@@ -509,19 +510,21 @@
             blocks.append(swap(moved, "dp", j) if j else moved)
         return blocks
 
-    arrived, pair_sums = [], []
-
-    def finish(batch, sums, after, results):
-        if batch == batches - 2:
-            after = [after, results[-1]]
-        if batch == batches - 1:
-            arrived.append(to_shards(results[: batches - 2]))
-            after = arrived[0][1:3]
+    pair_sums, early = [], []
+
+    def finish(batch, sums, after, results, last):
         sums, _ = lax.optimization_barrier((sums, (after, pair_sums[-1:])))
         rows_in = [part.reshape(-1, w_second.shape[0]) for part in sums]
         send, block = second(rows_in, b_first, goes[batch], w_second)
+        if batch == batches - 2:
+            ends = [last[0][-1], last[1][-1], results[-1]]
+            send, ends = lax.optimization_barrier((send, ends))
+            last[0][-1], last[1][-1], results[-1] = ends
         if batch == batches - 1:
-            send, results[-1] = lax.optimization_barrier((send, results[-1]))
+            early.extend(to_shards(results[: batches - 2]))
+            ends = [results[-1], *early[1:3]]
+            send, ends = lax.optimization_barrier((send, ends))
+            results[-1], *early[1:3] = ends
         wait = send
         block = add16(block, swap(send, "tensor", 1))
         pair_sums.append(block)
@@ -533,7 +536,7 @@
         return wait, block.reshape(dps, part * images, columns)
 
     held = line_sums(streams, "dp", finish)
-    arrived.append(to_shards(held[batches - 2 :]))
+    arrived = [early, to_shards(held[batches - 2 :])]
     visual = [[] for _ in range(tensors)]
     for group in (arrived[:-1], arrived[-1:]):
         group = jnp.concatenate([jnp.stack(blocks) for blocks in group], axis=1)

time: 221 us -> 216 us (0.977)
  waiting for transfers between devices: 76.2 us -> 65.6 us
  starting transfers between devices: 82 us -> 87.1 us
    ppermute x24, waiting for transfers between devices: 25.6 us -> 19.5 us  [line_sums(): came[s][w].append(lax.ppermute(value, axis, pairs))]
    ppermute x44, starting transfers between devices: 33.8 us -> 39 us  [swap(): return lax.ppermute(x, axis, [(a, a ^ k) for a in range(n)])]
    ppermute x44, waiting for transfers between devices: 50.6 us -> 46.1 us  [swap(): return lax.ppermute(x, axis, [(a, a ^ k) for a in range(n)])]
  transfers between devices with their start and end apart: 68 -> 68, of which waited for: 29 -> 26; matrix products, arithmetic and copies ran while one was open for 4% -> 4% of each run, Pallas kernels for 17% -> 18%
where the time goes in v2:
time: 216 us; the launch traced here: 215 us
  starting transfers between devices  87.1 us (40%)
  waiting for transfers between devices  65.6 us (30%)
  Pallas kernels  46.5 us (22%)
  local copies, waits for them, and re-layouts  7.72 us (4%)
  other arithmetic  5.68 us (3%)
  between operations  2.46 us (1%)
    ppermute x24, starting transfers between devices, line_sums(): came[s][w].append(lax.ppermute(value, axis, pairs))  48.2 us
    ppermute x44, waiting for transfers between devices, swap(): return lax.ppermute(x, axis, [(a, a ^ k) for a in range(n)])  46.1 us
    ppermute x44, starting transfers between devices, swap(): return lax.ppermute(x, axis, [(a, a ^ k) for a in range(n)])  39 us
    ppermute x24, waiting for transfers between devices, line_sums(): came[s][w].append(lax.ppermute(value, axis, pairs))  19.5 us
    pallas_call x4, Pallas kernels, second(): pl.pallas_call(functools.partial(second_kernel, count), out_shape=[out, o...  17.2 us
    pallas_call x1, Pallas kernels, attend(): pl.pallas_call(attend_kernel, out_shape=[bf16(rows // parts, cols)] * par...  14.1 us
    pallas_call x2, Pallas kernels, first(): pl.pallas_call(functools.partial(first_kernel, len(groups), batches, imag...  7.12 us
    pallas_call x1, Pallas kernels, project(): pl.pallas_call(functools.partial(project_kernel, count, splits), out_shap...  4.75 us
  transfers between devices with their start and end apart: 68, of which 26 were waited for; matrix products, arithmetic and copies ran while one was open for 4% of the time, Pallas kernels for 18%

profile of v2, /device:TPU:0, one launch (start us, length us, event | category | flops | bytes accessed | tf_op | source)
XLA Modules:
  0.0 215.1 jit_solution(855955044804095925)
XLA Ops:
  3.0 14.1 %shard_map.136 = (bf16[256,320]{1,0:T(8,128)(2,1)}, bf16[256,320]{1,0:T(8,128)(2,1)}, bf16[256,320]{1,0:T(8,128)(2,1)}, bf16[256,320]{1,0:T(8,128)(2,1)}) custom-call(s32[1,2]{1,0:T(1,128)} %grid_ref.1, bf16[1024,1280]{1,0:T(8,128)(2,1)} %x_hbm.3, f32[1280]{0:T(1024)} %gain_ref.2, bf16[3,320,1280]{2,1,0:T(8,128)(2,1)} %bitcast.187, f32[3,320]{1,0:T(4,128)} %b_ref.1), custom_call_target="tpu_custom_call" | custom-call | flops 3858759680 | bytes 7700480 | tf_op jit(solution)/shard_map/pallas_call | solution.py:200
  30.8 3.5 %collective-permute-done.4 = s32[256]{0:T(256)S(1)} collective-permute-done((s32[256]{0:T(256)S(1)}, s32[256]{0:T(256)S(1)}, u32[]{:S(2)}, u32[]{:S(2)}) %collective-permute-start.4) | collective-permute-done | bytes 1056 | tf_op jit(solution)/shard_map/ppermute | solution.py:34
  39.3 4.7 %shard_map.137 = (bf16[64,1280]{1,0:T(8,128)(2,1)}, bf16[64,1280]{1,0:T(8,128)(2,1)}, bf16[64,1280]{1,0:T(8,128)(2,1)}, bf16[64,1280]{1,0:T(8,128)(2,1)}) custom-call(bf16[1024,1280]{1,0:T(8,128)(2,1)} %x_hbm.3, f32[1280]{0:T(1024)S(1)} %copy-done.6, f32[1280]{0:T(1024)S(1)} %copy-done.7, bf16[256,320]{1,0:T(8,128)(2,1)S(1)} %copy-done.2, ...), custom_call_target="tpu_custom_call" | custom-call | flops 838860800 | bytes 5242880 | tf_op jit(solution)/shard_map/pallas_call | solution.py:262
  46.4 3.6 %collective-permute-start.13 = (bf16[64,1280]{1,0:T(8,128)(2,1)}, bf16[64,1280]{1,0:T(8,128)(2,1)S(1)}, u32[]{:S(2)}, u32[]{:S(2)}) collective-permute-start(bf16[64,1280]{1,0:T(8,128)(2,1)} %get-tuple-element.77), channel_id=1, source_target_pairs={{0,12},{4,8},{8,4},{12,0},{1,13},{5,9},{9,5},{13,1},{2,14},{6,10},... | collective-permute-start | bytes 491528 | tf_op jit(solution)/shard_map/ppermute | solution.py:34
  51.2 8.0 %collective-permute-done.12.rest_2_ = bf16[64,1280]{1,0:T(8,128)(2,1)S(1)} collective-permute-done((bf16[64,1280]{1,0:T(8,128)(2,1)}, bf16[64,1280]{1,0:T(8,128)(2,1)S(1)}, u32[]{:S(2)}, u32[]{:S(2)}) %collective-permute-start.12) | collective-permute-done | bytes 163872 | tf_op jit(solution)/shard_map/ppermute | solution.py:34
  63.8 3.4 %shard_map.138 = (bf16[4,2,64,1280]{3,2,1,0:T(8,128)(2,1)S(1)}, bf16[4,2,64,1280]{3,2,1,0:T(8,128)(2,1)S(1)}) custom-call(bf16[1280,1280]{1,0:T(8,128)(2,1)S(1)} %copy-done.9, bf16[64,1280]{1,0:T(8,128)(2,1)} %get-tuple-element.73.rest_0_, bf16[64,1280]{1,0:T(8,128)(2,1)S(1)} %collective-permute-done.9.rest_1_, ...), custom_call_target="tpu_custom_call" | custom-call | flops 1677721600 | bytes 7208960 | tf_op jit(solution)/shard_map/pallas_call | solution.py:317
  67.3 3.7 %collective-permute-start.18 = (bf16[2,64,1280]{2,1,0:T(8,128)(2,1)S(1)}, bf16[2,64,1280]{2,1,0:T(8,128)(2,1)S(1)}, u32[]{:S(2)}, u32[]{:S(2)}) collective-permute-start(bf16[2,64,1280]{2,1,0:T(8,128)(2,1)S(1)} %slice_bitcast_fusion.3), channel_id=1, source_target_pairs={{0,4},{1,5},{2,6},{3,7},{16,20},{17,21},{18,22},{19,23}} | collective-permute-start | bytes 983048 | tf_op jit(solution)/shard_map/ppermute | solution.py:85
  73.0 3.7 %shard_map.139 = (bf16[4,2,64,1280]{3,2,1,0:T(8,128)(2,1)S(1)}, bf16[4,2,64,1280]{3,2,1,0:T(8,128)(2,1)S(1)}) custom-call(bf16[1280,1280]{1,0:T(8,128)(2,1)S(1)} %copy-done.10, bf16[64,1280]{1,0:T(8,128)(2,1)S(1)} %collective-permute-done.10.rest_0_, bf16[64,1280]{1,0:T(8,128)(2,1)S(1)} %collective-permute-done.11.rest_1_, ...), custom_call_target="tpu_custom_call" | custom-call | flops 1677721600 | bytes 7208960 | tf_op jit(solution)/shard_map/pallas_call | solution.py:317
  79.6 3.5 %collective-permute-start.19 = (bf16[2,64,1280]{2,1,0:T(8,128)(2,1)S(1)}, bf16[2,64,1280]{2,1,0:T(8,128)(2,1)S(1)}, u32[]{:S(2)}, u32[]{:S(2)}) collective-permute-start(bf16[2,64,1280]{2,1,0:T(8,128)(2,1)S(1)} %fusion), channel_id=1, source_target_pairs={{0,4},{4,8},{1,5},{5,9},{2,6},{6,10},{3,7},{7,11},{16,20},{20,24},... | collective-permute-start | bytes 983048 | tf_op jit(solution)/shard_map/ppermute | solution.py:85
  86.9 4.4 %collective-permute-start.31 = (bf16[2,64,1280]{2,1,0:T(8,128)(2,1)S(1)}, bf16[2,64,1280]{2,1,0:T(8,128)(2,1)S(1)}, u32[]{:S(2)}, u32[]{:S(2)}) collective-permute-start(bf16[2,64,1280]{2,1,0:T(8,128)(2,1)S(1)} %fusion.2), channel_id=1, source_target_pairs={{0,4},{4,8},{1,5},{5,9},{2,6},{6,10},{3,7},{7,11},{16,20},{20,24},... | collective-permute-start | bytes 983048 | tf_op jit(solution)/shard_map/ppermute | solution.py:85
  93.9 4.4 %collective-permute-start.20 = (bf16[2,64,1280]{2,1,0:T(8,128)(2,1)S(1)}, bf16[2,64,1280]{2,1,0:T(8,128)(2,1)S(1)}, u32[]{:S(2)}, u32[]{:S(2)}) collective-permute-start(bf16[2,64,1280]{2,1,0:T(8,128)(2,1)S(1)} %fusion.6), channel_id=1, source_target_pairs={{0,4},{4,8},{8,12},{1,5},{5,9},{9,13},{2,6},{6,10},{10,14},{3,7},{... | collective-permute-start | bytes 983048 | tf_op jit(solution)/shard_map/ppermute | solution.py:85
  101.0 4.4 %collective-permute-start.32 = (bf16[2,64,1280]{2,1,0:T(8,128)(2,1)S(1)}, bf16[2,64,1280]{2,1,0:T(8,128)(2,1)S(1)}, u32[]{:S(2)}, u32[]{:S(2)}) collective-permute-start(bf16[2,64,1280]{2,1,0:T(8,128)(2,1)S(1)} %fusion.12), channel_id=1, source_target_pairs={{0,4},{4,8},{8,12},{1,5},{5,9},{9,13},{2,6},{6,10},{10,14},{3,7},{... | collective-permute-start | bytes 983048 | tf_op jit(solution)/shard_map/ppermute | solution.py:85
  108.6 4.1 %collective-permute-start.36 = (bf16[2,64,1280]{2,1,0:T(8,128)(2,1)S(1)}, bf16[2,64,1280]{2,1,0:T(8,128)(2,1)S(1)}, u32[]{:S(2)}, u32[]{:S(2)}) collective-permute-start(bf16[2,64,1280]{2,1,0:T(8,128)(2,1)S(1)} %get-tuple-element.126), channel_id=1, source_target_pairs={{0,4},{4,8},{8,12},{1,5},{5,9},{9,13},{2,6},{6,10},{10,14},{3,7},{... | collective-permute-start | bytes 983048 | tf_op jit(solution)/shard_map/ppermute | solution.py:85
  115.6 5.3 %collective-permute-start.42 = (bf16[2,64,1280]{2,1,0:T(8,128)(2,1)S(1)}, bf16[2,64,1280]{2,1,0:T(8,128)(2,1)S(1)}, u32[]{:S(2)}, u32[]{:S(2)}) collective-permute-start(bf16[2,64,1280]{2,1,0:T(8,128)(2,1)S(1)} %get-tuple-element.124), channel_id=1, source_target_pairs={{0,4},{4,8},{8,12},{1,5},{5,9},{9,13},{2,6},{6,10},{10,14},{3,7},{... | collective-permute-start | bytes 983048 | tf_op jit(solution)/shard_map/ppermute | solution.py:85
  128.1 4.3 %shard_map.140 = (bf16[128,2048]{1,0:T(8,128)(2,1)S(1)}, bf16[128,2048]{1,0:T(8,128)(2,1)S(1)}) custom-call(f32[1280]{0:T(1024)S(1)} %copy-done.5, s32[1,256]{1,0:T(1,128)S(1)} %get-tuple-element.155.goes_ref, bf16[1280,2048]{1,0:T(8,128)(2,1)} %w_hbm.7, f32[128,1280]{1,0:T(8,128)S(1)} %bitcast.157, f32[128,1280]{1,0:T(8,128)S(1)} %bitcast.158), custom_call_target="tpu_custom_call" | custom-call | flops 1342177280 | bytes 5242880 | tf_op jit(solution)/shard_map/pallas_call | solution.py:358
  135.7 3.8 %collective-permute-done.41 = bf16[2,64,1280]{2,1,0:T(8,128)(2,1)S(1)} collective-permute-done((bf16[2,64,1280]{2,1,0:T(8,128)(2,1)S(1)}, bf16[2,64,1280]{2,1,0:T(8,128)(2,1)S(1)}, u32[]{:S(2)}, u32[]{:S(2)}) %collective-permute-start.41) | collective-permute-done | bytes 327712 | tf_op jit(solution)/shard_map/ppermute | solution.py:85
  142.0 4.3 %shard_map.141 = (bf16[128,2048]{1,0:T(8,128)(2,1)S(1)}, bf16[128,2048]{1,0:T(8,128)(2,1)S(1)}) custom-call(f32[1280]{0:T(1024)S(1)} %copy-done.5, s32[1,256]{1,0:T(1,128)S(1)} %get-tuple-element.153.goes_ref, bf16[1280,2048]{1,0:T(8,128)(2,1)} %w_hbm.7, f32[128,1280]{1,0:T(8,128)S(1)} %bitcast.156, f32[128,1280]{1,0:T(8,128)S(1)} %bitcast.161), custom_call_target="tpu_custom_call" | custom-call | flops 1342177280 | bytes 5242880 | tf_op jit(solution)/shard_map/pallas_call | solution.py:358
  155.1 4.3 %shard_map.142 = (bf16[128,2048]{1,0:T(8,128)(2,1)S(1)}, bf16[128,2048]{1,0:T(8,128)(2,1)S(1)}) custom-call(f32[1280]{0:T(1024)S(1)} %copy-done.5, s32[1,256]{1,0:T(1,128)S(1)} %get-tuple-element.154.goes_ref, bf16[1280,2048]{1,0:T(8,128)(2,1)} %w_hbm.7, f32[128,1280]{1,0:T(8,128)S(1)} %bitcast.154, f32[128,1280]{1,0:T(8,128)S(1)} %bitcast.160), custom_call_target="tpu_custom_call" | custom-call | flops 1342177280 | bytes 5242880 | tf_op jit(solution)/shard_map/pallas_call | solution.py:358
  159.5 4.6 %collective-permute-done.51 = bf16[64,2048]{1,0:T(8,128)(2,1)S(1)} collective-permute-done((bf16[64,2048]{1,0:T(8,128)(2,1)S(1)}, bf16[64,2048]{1,0:T(8,128)(2,1)S(1)}, u32[]{:S(2)}, u32[]{:S(2)}) %collective-permute-start.51) | collective-permute-done | bytes 262176 | tf_op jit(solution)/shard_map/ppermute | solution.py:34
  164.4 3.7 %collective-permute-start.54 = (bf16[2,16,2048]{2,1,0:T(8,128)(2,1)S(1)}, bf16[2,16,2048]{2,1,0:T(8,128)(2,1)S(1)}, u32[]{:S(2)}, u32[]{:S(2)}) collective-permute-start(bf16[2,16,2048]{2,1,0:T(8,128)(2,1)S(1)} %get-tuple-element.144), channel_id=1, source_target_pairs={{0,4},{4,0},{8,12},{12,8},{1,5},{5,1},{9,13},{13,9},{2,6},{6,2},{1... | collective-permute-start | bytes 393224 | tf_op jit(solution)/shard_map/ppermute | solution.py:34
  171.1 4.3 %shard_map.143 = (bf16[128,2048]{1,0:T(8,128)(2,1)S(1)}, bf16[128,2048]{1,0:T(8,128)(2,1)S(1)}) custom-call(f32[1280]{0:T(1024)S(1)} %copy-done.5, s32[1,256]{1,0:T(1,128)S(1)} %get-tuple-element.152.goes_ref, bf16[1280,2048]{1,0:T(8,128)(2,1)} %w_hbm.7, f32[128,1280]{1,0:T(8,128)S(1)} %bitcast.155, f32[128,1280]{1,0:T(8,128)S(1)} %bitcast.159), custom_call_target="tpu_custom_call" | custom-call | flops 1342177280 | bytes 5242880 | tf_op jit(solution)/shard_map/pallas_call | solution.py:358
  181.4 5.3 %collective-permute-done.56 = bf16[2,16,2048]{2,1,0:T(8,128)(2,1)S(1)} collective-permute-done((bf16[2,16,2048]{2,1,0:T(8,128)(2,1)S(1)}, bf16[2,16,2048]{2,1,0:T(8,128)(2,1)S(1)}, u32[]{:S(2)}, u32[]{:S(2)}) %collective-permute-start.56) | collective-permute-done | bytes 131104 | tf_op jit(solution)/shard_map/ppermute | solution.py:34
  196.1 7.1 %collective-permute-done.60 = bf16[2,16,2048]{2,1,0:T(8,128)(2,1)S(1)} collective-permute-done((bf16[2,16,2048]{2,1,0:T(8,128)(2,1)S(1)}, bf16[2,16,2048]{2,1,0:T(8,128)(2,1)S(1)}, u32[]{:S(2)}, u32[]{:S(2)}) %collective-permute-start.60) | collective-permute-done | bytes 131104 | tf_op jit(solution)/shard_map/ppermute | solution.py:34
  205.2 4.5 %collective-permute-done.65 = bf16[1,32,2048]{2,1,0:T(8,128)(2,1)S(1)} collective-permute-done((bf16[1,32,2048]{2,1,0:T(8,128)(2,1)S(1)}, bf16[1,32,2048]{2,1,0:T(8,128)(2,1)S(1)}, u32[]{:S(2)}, u32[]{:S(2)}) %collective-permute-start.65) | collective-permute-done | bytes 131104 | tf_op jit(solution)/shard_map/ppermute | solution.py:34
  (215 shorter events, 95.6 us)
Async XLA Ops:
  0.0 22.2 %collective-permute-start.1 = (bf16[320,1280]{1,0:T(8,128)(2,1)}, bf16[320,1280]{1,0:T(8,128)(2,1)S(1)}, u32[]{:S(2)}, u32[]{:S(2)}) collective-permute-start(bf16[320,1280]{1,0:T(8,128)(2,1)} %rest_4_), channel_id=1, source_target_pairs={{0,2},{1,3},{2,0},{3,1},{4,6},{5,7},{6,4},{7,5},{8,10},{9,11},{10,... | collective-permute-start | bytes 2457608 | tf_op jit(solution)/shard_map/ppermute | solution.py:34
  17.2 20.2 %collective-permute-start.5 = (bf16[256,320]{1,0:T(8,128)(2,1)}, bf16[256,320]{1,0:T(8,128)(2,1)}, u32[]{:S(2)}, u32[]{:S(2)}) collective-permute-start(bf16[256,320]{1,0:T(8,128)(2,1)} %get-tuple-element.70), channel_id=1, source_target_pairs={{0,2},{1,3},{2,0},{3,1},{4,6},{5,7},{6,4},{7,5},{8,10},{9,11},{10,... | collective-permute-start | bytes 491528 | tf_op jit(solution)/shard_map/ppermute | solution.py:34
  17.3 20.1 %collective-permute-start.6 = (bf16[256,320]{1,0:T(8,128)(2,1)}, bf16[256,320]{1,0:T(8,128)(2,1)}, u32[]{:S(2)}, u32[]{:S(2)}) collective-permute-start(bf16[256,320]{1,0:T(8,128)(2,1)} %get-tuple-element.71), channel_id=1, source_target_pairs={{0,3},{1,2},{2,1},{3,0},{4,7},{5,6},{6,5},{7,4},{8,11},{9,10},{10,... | collective-permute-start | bytes 491528 | tf_op jit(solution)/shard_map/ppermute | solution.py:34
  45.7 13.5 %collective-permute-start.12 = (bf16[64,1280]{1,0:T(8,128)(2,1)}, bf16[64,1280]{1,0:T(8,128)(2,1)S(1)}, u32[]{:S(2)}, u32[]{:S(2)}) collective-permute-start(bf16[64,1280]{1,0:T(8,128)(2,1)} %get-tuple-element.76), channel_id=1, source_target_pairs={{0,8},{4,12},{8,0},{12,4},{1,9},{5,13},{9,1},{13,5},{2,10},{6,14},... | collective-permute-start | bytes 491528 | tf_op jit(solution)/shard_map/ppermute | solution.py:34
  46.4 12.8 %collective-permute-start.13 = (bf16[64,1280]{1,0:T(8,128)(2,1)}, bf16[64,1280]{1,0:T(8,128)(2,1)S(1)}, u32[]{:S(2)}, u32[]{:S(2)}) collective-permute-start(bf16[64,1280]{1,0:T(8,128)(2,1)} %get-tuple-element.77), channel_id=1, source_target_pairs={{0,12},{4,8},{8,4},{12,0},{1,13},{5,9},{9,5},{13,1},{2,14},{6,10},... | collective-permute-start | bytes 491528 | tf_op jit(solution)/shard_map/ppermute | solution.py:34
  78.8 12.5 %collective-permute-start.33 = (bf16[2,64,1280]{2,1,0:T(8,128)(2,1)S(1)}, bf16[2,64,1280]{2,1,0:T(8,128)(2,1)S(1)}, u32[]{:S(2)}, u32[]{:S(2)}) collective-permute-start(bf16[2,64,1280]{2,1,0:T(8,128)(2,1)S(1)} %slice_bitcast_fusion), channel_id=1, source_target_pairs={{12,8},{13,9},{14,10},{15,11},{28,24},{29,25},{30,26},{31,27}} | collective-permute-start | bytes 983048 | tf_op jit(solution)/shard_map/ppermute | solution.py:85
  79.6 14.2 %collective-permute-start.19 = (bf16[2,64,1280]{2,1,0:T(8,128)(2,1)S(1)}, bf16[2,64,1280]{2,1,0:T(8,128)(2,1)S(1)}, u32[]{:S(2)}, u32[]{:S(2)}) collective-permute-start(bf16[2,64,1280]{2,1,0:T(8,128)(2,1)S(1)} %fusion), channel_id=1, source_target_pairs={{0,4},{4,8},{1,5},{5,9},{2,6},{6,10},{3,7},{7,11},{16,20},{20,24},... | collective-permute-start | bytes 983048 | tf_op jit(solution)/shard_map/ppermute | solution.py:85
  83.2 15.1 %collective-permute-start.22 = (bf16[2,64,1280]{2,1,0:T(8,128)(2,1)S(1)}, bf16[2,64,1280]{2,1,0:T(8,128)(2,1)S(1)}, u32[]{:S(2)}, u32[]{:S(2)}) collective-permute-start(bf16[2,64,1280]{2,1,0:T(8,128)(2,1)S(1)} %fusion.4), channel_id=1, source_target_pairs={{12,8},{8,4},{13,9},{9,5},{14,10},{10,6},{15,11},{11,7},{28,24},{2... | collective-permute-start | bytes 983048 | tf_op jit(solution)/shard_map/ppermute | solution.py:85
  86.9 14.0 %collective-permute-start.31 = (bf16[2,64,1280]{2,1,0:T(8,128)(2,1)S(1)}, bf16[2,64,1280]{2,1,0:T(8,128)(2,1)S(1)}, u32[]{:S(2)}, u32[]{:S(2)}) collective-permute-start(bf16[2,64,1280]{2,1,0:T(8,128)(2,1)S(1)} %fusion.2), channel_id=1, source_target_pairs={{0,4},{4,8},{1,5},{5,9},{2,6},{6,10},{3,7},{7,11},{16,20},{20,24},... | collective-permute-start | bytes 983048 | tf_op jit(solution)/shard_map/ppermute | solution.py:85
  91.4 14.0 %collective-permute-start.34 = (bf16[2,64,1280]{2,1,0:T(8,128)(2,1)S(1)}, bf16[2,64,1280]{2,1,0:T(8,128)(2,1)S(1)}, u32[]{:S(2)}, u32[]{:S(2)}) collective-permute-start(bf16[2,64,1280]{2,1,0:T(8,128)(2,1)S(1)} %fusion.10), channel_id=1, source_target_pairs={{12,8},{8,4},{13,9},{9,5},{14,10},{10,6},{15,11},{11,7},{28,24},{2... | collective-permute-start | bytes 983048 | tf_op jit(solution)/shard_map/ppermute | solution.py:85
  93.9 14.0 %collective-permute-start.20 = (bf16[2,64,1280]{2,1,0:T(8,128)(2,1)S(1)}, bf16[2,64,1280]{2,1,0:T(8,128)(2,1)S(1)}, u32[]{:S(2)}, u32[]{:S(2)}) collective-permute-start(bf16[2,64,1280]{2,1,0:T(8,128)(2,1)S(1)} %fusion.6), channel_id=1, source_target_pairs={{0,4},{4,8},{8,12},{1,5},{5,9},{9,13},{2,6},{6,10},{10,14},{3,7},{... | collective-permute-start | bytes 983048 | tf_op jit(solution)/shard_map/ppermute | solution.py:85
  101.0 14.0 %collective-permute-start.32 = (bf16[2,64,1280]{2,1,0:T(8,128)(2,1)S(1)}, bf16[2,64,1280]{2,1,0:T(8,128)(2,1)S(1)}, u32[]{:S(2)}, u32[]{:S(2)}) collective-permute-start(bf16[2,64,1280]{2,1,0:T(8,128)(2,1)S(1)} %fusion.12), channel_id=1, source_target_pairs={{0,4},{4,8},{8,12},{1,5},{5,9},{9,13},{2,6},{6,10},{10,14},{3,7},{... | collective-permute-start | bytes 983048 | tf_op jit(solution)/shard_map/ppermute | solution.py:85
  108.6 13.6 %collective-permute-start.36 = (bf16[2,64,1280]{2,1,0:T(8,128)(2,1)S(1)}, bf16[2,64,1280]{2,1,0:T(8,128)(2,1)S(1)}, u32[]{:S(2)}, u32[]{:S(2)}) collective-permute-start(bf16[2,64,1280]{2,1,0:T(8,128)(2,1)S(1)} %get-tuple-element.126), channel_id=1, source_target_pairs={{0,4},{4,8},{8,12},{1,5},{5,9},{9,13},{2,6},{6,10},{10,14},{3,7},{... | collective-permute-start | bytes 983048 | tf_op jit(solution)/shard_map/ppermute | solution.py:85
  112.7 12.7 %collective-permute-start.37 = (bf16[2,64,1280]{2,1,0:T(8,128)(2,1)S(1)}, bf16[2,64,1280]{2,1,0:T(8,128)(2,1)S(1)}, u32[]{:S(2)}, u32[]{:S(2)}) collective-permute-start(bf16[2,64,1280]{2,1,0:T(8,128)(2,1)S(1)} %get-tuple-element.151), channel_id=1, source_target_pairs={{12,8},{8,4},{4,0},{13,9},{9,5},{5,1},{14,10},{10,6},{6,2},{15,11}... | collective-permute-start | bytes 983048 | tf_op jit(solution)/shard_map/ppermute | solution.py:85
  115.6 16.8 %collective-permute-start.42 = (bf16[2,64,1280]{2,1,0:T(8,128)(2,1)S(1)}, bf16[2,64,1280]{2,1,0:T(8,128)(2,1)S(1)}, u32[]{:S(2)}, u32[]{:S(2)}) collective-permute-start(bf16[2,64,1280]{2,1,0:T(8,128)(2,1)S(1)} %get-tuple-element.124), channel_id=1, source_target_pairs={{0,4},{4,8},{8,12},{1,5},{5,9},{9,13},{2,6},{6,10},{10,14},{3,7},{... | collective-permute-start | bytes 983048 | tf_op jit(solution)/shard_map/ppermute | solution.py:85
  126.5 13.0 %collective-permute-start.41 = (bf16[2,64,1280]{2,1,0:T(8,128)(2,1)S(1)}, bf16[2,64,1280]{2,1,0:T(8,128)(2,1)S(1)}, u32[]{:S(2)}, u32[]{:S(2)}) collective-permute-start(bf16[2,64,1280]{2,1,0:T(8,128)(2,1)S(1)} %get-tuple-element.150), channel_id=1, source_target_pairs={{8,4},{4,0},{9,5},{5,1},{10,6},{6,2},{11,7},{7,3},{24,20},{20,16},... | collective-permute-start | bytes 983048 | tf_op jit(solution)/shard_map/ppermute | solution.py:85
  133.3 14.5 %collective-permute-start.45 = (bf16[2,64,1280]{2,1,0:T(8,128)(2,1)S(1)}, bf16[2,64,1280]{2,1,0:T(8,128)(2,1)S(1)}, u32[]{:S(2)}, u32[]{:S(2)}) collective-permute-start(bf16[2,64,1280]{2,1,0:T(8,128)(2,1)S(1)} %add_convert_fusion.4), channel_id=1, source_target_pairs={{8,4},{4,0},{9,5},{5,1},{10,6},{6,2},{11,7},{7,3},{24,20},{20,16},... | collective-permute-start | bytes 983048 | tf_op jit(solution)/shard_map/ppermute | solution.py:85
  135.0 12.9 %collective-permute-start.43 = (bf16[2,64,1280]{2,1,0:T(8,128)(2,1)S(1)}, bf16[2,64,1280]{2,1,0:T(8,128)(2,1)S(1)}, u32[]{:S(2)}, u32[]{:S(2)}) collective-permute-start(bf16[2,64,1280]{2,1,0:T(8,128)(2,1)S(1)} %get-tuple-element.118), channel_id=1, source_target_pairs={{4,8},{8,12},{5,9},{9,13},{6,10},{10,14},{7,11},{11,15},{20,24},{2... | collective-permute-start | bytes 983048 | tf_op jit(solution)/shard_map/ppermute | solution.py:85
  140.6 14.2 %collective-permute-start.47 = (bf16[2,64,1280]{2,1,0:T(8,128)(2,1)S(1)}, bf16[2,64,1280]{2,1,0:T(8,128)(2,1)S(1)}, u32[]{:S(2)}, u32[]{:S(2)}) collective-permute-start(bf16[2,64,1280]{2,1,0:T(8,128)(2,1)S(1)} %get-tuple-element.148), channel_id=1, source_target_pairs={{4,0},{5,1},{6,2},{7,3},{20,16},{21,17},{22,18},{23,19}} | collective-permute-start | bytes 983048 | tf_op jit(solution)/shard_map/ppermute | solution.py:85
  147.9 16.3 %collective-permute-start.50 = (bf16[2,64,1280]{2,1,0:T(8,128)(2,1)S(1)}, bf16[2,64,1280]{2,1,0:T(8,128)(2,1)S(1)}, u32[]{:S(2)}, u32[]{:S(2)}) collective-permute-start(bf16[2,64,1280]{2,1,0:T(8,128)(2,1)S(1)} %fusion.11), channel_id=1, source_target_pairs={{4,0},{5,1},{6,2},{7,3},{20,16},{21,17},{22,18},{23,19}} | collective-permute-start | bytes 983048 | tf_op jit(solution)/shard_map/ppermute | solution.py:85
  149.5 14.6 %collective-permute-start.49 = (bf16[2,64,1280]{2,1,0:T(8,128)(2,1)S(1)}, bf16[2,64,1280]{2,1,0:T(8,128)(2,1)S(1)}, u32[]{:S(2)}, u32[]{:S(2)}) collective-permute-start(bf16[2,64,1280]{2,1,0:T(8,128)(2,1)S(1)} %get-tuple-element.116), channel_id=1, source_target_pairs={{8,12},{9,13},{10,14},{11,15},{24,28},{25,29},{26,30},{27,31}} | collective-permute-start | bytes 983048 | tf_op jit(solution)/shard_map/ppermute | solution.py:85
  150.5 13.8 %collective-permute-start.39 = (bf16[64,2048]{1,0:T(8,128)(2,1)S(1)}, bf16[64,2048]{1,0:T(8,128)(2,1)S(1)}, u32[]{:S(2)}, u32[]{:S(2)}) collective-permute-start(bf16[64,2048]{1,0:T(8,128)(2,1)S(1)} %slice.139), channel_id=1, source_target_pairs={{0,2},{1,3},{2,0},{3,1},{4,6},{5,7},{6,4},{7,5},{8,10},{9,11},{10,... | collective-permute-start | bytes 786440 | tf_op jit(solution)/shard_map/ppermute | solution.py:34
  151.1 12.9 %collective-permute-start.51 = (bf16[64,2048]{1,0:T(8,128)(2,1)S(1)}, bf16[64,2048]{1,0:T(8,128)(2,1)S(1)}, u32[]{:S(2)}, u32[]{:S(2)}) collective-permute-start(bf16[64,2048]{1,0:T(8,128)(2,1)S(1)} %slice.141), channel_id=1, source_target_pairs={{0,2},{1,3},{2,0},{3,1},{4,6},{5,7},{6,4},{7,5},{8,10},{9,11},{10,... | collective-permute-start | bytes 786440 | tf_op jit(solution)/shard_map/ppermute | solution.py:34
  164.4 14.4 %collective-permute-start.54 = (bf16[2,16,2048]{2,1,0:T(8,128)(2,1)S(1)}, bf16[2,16,2048]{2,1,0:T(8,128)(2,1)S(1)}, u32[]{:S(2)}, u32[]{:S(2)}) collective-permute-start(bf16[2,16,2048]{2,1,0:T(8,128)(2,1)S(1)} %get-tuple-element.144), channel_id=1, source_target_pairs={{0,4},{4,0},{8,12},{12,8},{1,5},{5,1},{9,13},{13,9},{2,6},{6,2},{1... | collective-permute-start | bytes 393224 | tf_op jit(solution)/shard_map/ppermute | solution.py:34
  (57 other events, 529.6 us)

commit v3 on v2

--- a/solution.py
+++ b/solution.py
@@ -262,7 +262,7 @@
     return pl.pallas_call(
         functools.partial(project_kernel, count, splits),
         out_shape=[bf16(rows // MERGE, width)] * MERGE,
-        in_specs=[anywhere(), vmem(), vmem()] + [anywhere()] * (2 * count),
+        in_specs=[hbm(), vmem(), vmem()] + ([hbm()] + [anywhere()] * (count - 1)) * 2,
         out_specs=[hbm()] * MERGE,
         scratch_shapes=[
             bf16_scratch(rows, width),
@@ -472,7 +472,7 @@
 
     blocks = [swap(block, "tensor", k) if k else block for k, block in enumerate(blocks)]
     blocks[1], proj_high = lax.optimization_barrier((blocks[1], proj_high))
-    goes, hit = places(proj_high[tensors // 2])
+    goes, hit = places(blocks[1])
     proj_blocks = {}
     for k, high in proj_high.items():
         for j, block in enumerate(gather_low(high, "tensor", tensors // 2)):

time: 216 us -> 216 us (level)
  no operation moved by 1% of the time
where the time goes in v3:
time: 216 us; the launch traced here: 215 us
  starting transfers between devices  87.1 us (40%)
  waiting for transfers between devices  65.6 us (30%)
  Pallas kernels  46.5 us (22%)
  local copies, waits for them, and re-layouts  7.72 us (4%)
  other arithmetic  5.68 us (3%)
  between operations  2.47 us (1%)
    ppermute x24, starting transfers between devices, line_sums(): came[s][w].append(lax.ppermute(value, axis, pairs))  48.2 us
    ppermute x44, waiting for transfers between devices, swap(): return lax.ppermute(x, axis, [(a, a ^ k) for a in range(n)])  46.1 us
    ppermute x44, starting transfers between devices, swap(): return lax.ppermute(x, axis, [(a, a ^ k) for a in range(n)])  39 us
    ppermute x24, waiting for transfers between devices, line_sums(): came[s][w].append(lax.ppermute(value, axis, pairs))  19.5 us
    pallas_call x4, Pallas kernels, second(): pl.pallas_call(functools.partial(second_kernel, count), out_shape=[out, o...  17.2 us
    pallas_call x1, Pallas kernels, attend(): pl.pallas_call(attend_kernel, out_shape=[bf16(rows // parts, cols)] * par...  14.1 us
    pallas_call x2, Pallas kernels, first(): pl.pallas_call(functools.partial(first_kernel, len(groups), batches, imag...  7.12 us
    pallas_call x1, Pallas kernels, project(): pl.pallas_call(functools.partial(project_kernel, count, splits), out_shap...  4.75 us
  transfers between devices with their start and end apart: 68, of which 26 were waited for; matrix products, arithmetic and copies ran while one was open for 4% of the time, Pallas kernels for 18%

profile of v3, /device:TPU:0, one launch (start us, length us, event | category | flops | bytes accessed | tf_op | source)
XLA Modules:
  0.0 215.1 jit_solution(1010877999903523921)
XLA Ops:
  3.0 14.1 %shard_map.136 = (bf16[256,320]{1,0:T(8,128)(2,1)}, bf16[256,320]{1,0:T(8,128)(2,1)}, bf16[256,320]{1,0:T(8,128)(2,1)}, bf16[256,320]{1,0:T(8,128)(2,1)}) custom-call(s32[1,2]{1,0:T(1,128)} %grid_ref.1, bf16[1024,1280]{1,0:T(8,128)(2,1)} %x_hbm.3, f32[1280]{0:T(1024)} %gain_ref.2, bf16[3,320,1280]{2,1,0:T(8,128)(2,1)} %bitcast.187, f32[3,320]{1,0:T(4,128)} %b_ref.1), custom_call_target="tpu_custom_call" | custom-call | flops 3858759680 | bytes 7700480 | tf_op jit(solution)/shard_map/pallas_call | solution.py:200
  30.8 3.5 %collective-permute-done.4 = s32[256]{0:T(256)S(1)} collective-permute-done((s32[256]{0:T(256)S(1)}, s32[256]{0:T(256)S(1)}, u32[]{:S(2)}, u32[]{:S(2)}) %collective-permute-start.4) | collective-permute-done | bytes 1056 | tf_op jit(solution)/shard_map/ppermute | solution.py:34
  39.3 4.7 %shard_map.137 = (bf16[64,1280]{1,0:T(8,128)(2,1)}, bf16[64,1280]{1,0:T(8,128)(2,1)}, bf16[64,1280]{1,0:T(8,128)(2,1)}, bf16[64,1280]{1,0:T(8,128)(2,1)}) custom-call(bf16[1024,1280]{1,0:T(8,128)(2,1)} %x_hbm.3, f32[1280]{0:T(1024)S(1)} %copy-done.6, f32[1280]{0:T(1024)S(1)} %copy-done.7, bf16[256,320]{1,0:T(8,128)(2,1)S(1)} %copy-done.2, ...), custom_call_target="tpu_custom_call" | custom-call | flops 838860800 | bytes 5242880 | tf_op jit(solution)/shard_map/pallas_call | solution.py:262
  46.4 3.6 %collective-permute-start.13 = (bf16[64,1280]{1,0:T(8,128)(2,1)}, bf16[64,1280]{1,0:T(8,128)(2,1)S(1)}, u32[]{:S(2)}, u32[]{:S(2)}) collective-permute-start(bf16[64,1280]{1,0:T(8,128)(2,1)} %get-tuple-element.77), channel_id=1, source_target_pairs={{0,12},{4,8},{8,4},{12,0},{1,13},{5,9},{9,5},{13,1},{2,14},{6,10},... | collective-permute-start | bytes 491528 | tf_op jit(solution)/shard_map/ppermute | solution.py:34
  51.2 8.0 %collective-permute-done.12.rest_2_ = bf16[64,1280]{1,0:T(8,128)(2,1)S(1)} collective-permute-done((bf16[64,1280]{1,0:T(8,128)(2,1)}, bf16[64,1280]{1,0:T(8,128)(2,1)S(1)}, u32[]{:S(2)}, u32[]{:S(2)}) %collective-permute-start.12) | collective-permute-done | bytes 163872 | tf_op jit(solution)/shard_map/ppermute | solution.py:34
  63.8 3.4 %shard_map.138 = (bf16[4,2,64,1280]{3,2,1,0:T(8,128)(2,1)S(1)}, bf16[4,2,64,1280]{3,2,1,0:T(8,128)(2,1)S(1)}) custom-call(bf16[1280,1280]{1,0:T(8,128)(2,1)S(1)} %copy-done.9, bf16[64,1280]{1,0:T(8,128)(2,1)} %get-tuple-element.73.rest_0_, bf16[64,1280]{1,0:T(8,128)(2,1)S(1)} %collective-permute-done.9.rest_1_, ...), custom_call_target="tpu_custom_call" | custom-call | flops 1677721600 | bytes 7208960 | tf_op jit(solution)/shard_map/pallas_call | solution.py:317
  67.3 3.7 %collective-permute-start.18 = (bf16[2,64,1280]{2,1,0:T(8,128)(2,1)S(1)}, bf16[2,64,1280]{2,1,0:T(8,128)(2,1)S(1)}, u32[]{:S(2)}, u32[]{:S(2)}) collective-permute-start(bf16[2,64,1280]{2,1,0:T(8,128)(2,1)S(1)} %slice_bitcast_fusion.3), channel_id=1, source_target_pairs={{0,4},{1,5},{2,6},{3,7},{16,20},{17,21},{18,22},{19,23}} | collective-permute-start | bytes 983048 | tf_op jit(solution)/shard_map/ppermute | solution.py:85
  73.0 3.7 %shard_map.139 = (bf16[4,2,64,1280]{3,2,1,0:T(8,128)(2,1)S(1)}, bf16[4,2,64,1280]{3,2,1,0:T(8,128)(2,1)S(1)}) custom-call(bf16[1280,1280]{1,0:T(8,128)(2,1)S(1)} %copy-done.10, bf16[64,1280]{1,0:T(8,128)(2,1)S(1)} %collective-permute-done.10.rest_0_, bf16[64,1280]{1,0:T(8,128)(2,1)S(1)} %collective-permute-done.11.rest_1_, ...), custom_call_target="tpu_custom_call" | custom-call | flops 1677721600 | bytes 7208960 | tf_op jit(solution)/shard_map/pallas_call | solution.py:317
  79.6 3.5 %collective-permute-start.19 = (bf16[2,64,1280]{2,1,0:T(8,128)(2,1)S(1)}, bf16[2,64,1280]{2,1,0:T(8,128)(2,1)S(1)}, u32[]{:S(2)}, u32[]{:S(2)}) collective-permute-start(bf16[2,64,1280]{2,1,0:T(8,128)(2,1)S(1)} %fusion), channel_id=1, source_target_pairs={{0,4},{4,8},{1,5},{5,9},{2,6},{6,10},{3,7},{7,11},{16,20},{20,24},... | collective-permute-start | bytes 983048 | tf_op jit(solution)/shard_map/ppermute | solution.py:85
  86.9 4.4 %collective-permute-start.31 = (bf16[2,64,1280]{2,1,0:T(8,128)(2,1)S(1)}, bf16[2,64,1280]{2,1,0:T(8,128)(2,1)S(1)}, u32[]{:S(2)}, u32[]{:S(2)}) collective-permute-start(bf16[2,64,1280]{2,1,0:T(8,128)(2,1)S(1)} %fusion.2), channel_id=1, source_target_pairs={{0,4},{4,8},{1,5},{5,9},{2,6},{6,10},{3,7},{7,11},{16,20},{20,24},... | collective-permute-start | bytes 983048 | tf_op jit(solution)/shard_map/ppermute | solution.py:85
  93.9 4.4 %collective-permute-start.20 = (bf16[2,64,1280]{2,1,0:T(8,128)(2,1)S(1)}, bf16[2,64,1280]{2,1,0:T(8,128)(2,1)S(1)}, u32[]{:S(2)}, u32[]{:S(2)}) collective-permute-start(bf16[2,64,1280]{2,1,0:T(8,128)(2,1)S(1)} %fusion.6), channel_id=1, source_target_pairs={{0,4},{4,8},{8,12},{1,5},{5,9},{9,13},{2,6},{6,10},{10,14},{3,7},{... | collective-permute-start | bytes 983048 | tf_op jit(solution)/shard_map/ppermute | solution.py:85
  101.0 4.4 %collective-permute-start.32 = (bf16[2,64,1280]{2,1,0:T(8,128)(2,1)S(1)}, bf16[2,64,1280]{2,1,0:T(8,128)(2,1)S(1)}, u32[]{:S(2)}, u32[]{:S(2)}) collective-permute-start(bf16[2,64,1280]{2,1,0:T(8,128)(2,1)S(1)} %fusion.12), channel_id=1, source_target_pairs={{0,4},{4,8},{8,12},{1,5},{5,9},{9,13},{2,6},{6,10},{10,14},{3,7},{... | collective-permute-start | bytes 983048 | tf_op jit(solution)/shard_map/ppermute | solution.py:85
  108.6 4.1 %collective-permute-start.36 = (bf16[2,64,1280]{2,1,0:T(8,128)(2,1)S(1)}, bf16[2,64,1280]{2,1,0:T(8,128)(2,1)S(1)}, u32[]{:S(2)}, u32[]{:S(2)}) collective-permute-start(bf16[2,64,1280]{2,1,0:T(8,128)(2,1)S(1)} %get-tuple-element.126), channel_id=1, source_target_pairs={{0,4},{4,8},{8,12},{1,5},{5,9},{9,13},{2,6},{6,10},{10,14},{3,7},{... | collective-permute-start | bytes 983048 | tf_op jit(solution)/shard_map/ppermute | solution.py:85
  115.6 5.3 %collective-permute-start.42 = (bf16[2,64,1280]{2,1,0:T(8,128)(2,1)S(1)}, bf16[2,64,1280]{2,1,0:T(8,128)(2,1)S(1)}, u32[]{:S(2)}, u32[]{:S(2)}) collective-permute-start(bf16[2,64,1280]{2,1,0:T(8,128)(2,1)S(1)} %get-tuple-element.124), channel_id=1, source_target_pairs={{0,4},{4,8},{8,12},{1,5},{5,9},{9,13},{2,6},{6,10},{10,14},{3,7},{... | collective-permute-start | bytes 983048 | tf_op jit(solution)/shard_map/ppermute | solution.py:85
  128.1 4.3 %shard_map.140 = (bf16[128,2048]{1,0:T(8,128)(2,1)S(1)}, bf16[128,2048]{1,0:T(8,128)(2,1)S(1)}) custom-call(f32[1280]{0:T(1024)S(1)} %copy-done.5, s32[1,256]{1,0:T(1,128)S(1)} %get-tuple-element.155.goes_ref, bf16[1280,2048]{1,0:T(8,128)(2,1)} %w_hbm.7, f32[128,1280]{1,0:T(8,128)S(1)} %bitcast.157, f32[128,1280]{1,0:T(8,128)S(1)} %bitcast.158), custom_call_target="tpu_custom_call" | custom-call | flops 1342177280 | bytes 5242880 | tf_op jit(solution)/shard_map/pallas_call | solution.py:358
  135.7 3.8 %collective-permute-done.41 = bf16[2,64,1280]{2,1,0:T(8,128)(2,1)S(1)} collective-permute-done((bf16[2,64,1280]{2,1,0:T(8,128)(2,1)S(1)}, bf16[2,64,1280]{2,1,0:T(8,128)(2,1)S(1)}, u32[]{:S(2)}, u32[]{:S(2)}) %collective-permute-start.41) | collective-permute-done | bytes 327712 | tf_op jit(solution)/shard_map/ppermute | solution.py:85
  142.0 4.3 %shard_map.141 = (bf16[128,2048]{1,0:T(8,128)(2,1)S(1)}, bf16[128,2048]{1,0:T(8,128)(2,1)S(1)}) custom-call(f32[1280]{0:T(1024)S(1)} %copy-done.5, s32[1,256]{1,0:T(1,128)S(1)} %get-tuple-element.153.goes_ref, bf16[1280,2048]{1,0:T(8,128)(2,1)} %w_hbm.7, f32[128,1280]{1,0:T(8,128)S(1)} %bitcast.156, f32[128,1280]{1,0:T(8,128)S(1)} %bitcast.161), custom_call_target="tpu_custom_call" | custom-call | flops 1342177280 | bytes 5242880 | tf_op jit(solution)/shard_map/pallas_call | solution.py:358
  155.1 4.3 %shard_map.142 = (bf16[128,2048]{1,0:T(8,128)(2,1)S(1)}, bf16[128,2048]{1,0:T(8,128)(2,1)S(1)}) custom-call(f32[1280]{0:T(1024)S(1)} %copy-done.5, s32[1,256]{1,0:T(1,128)S(1)} %get-tuple-element.154.goes_ref, bf16[1280,2048]{1,0:T(8,128)(2,1)} %w_hbm.7, f32[128,1280]{1,0:T(8,128)S(1)} %bitcast.154, f32[128,1280]{1,0:T(8,128)S(1)} %bitcast.160), custom_call_target="tpu_custom_call" | custom-call | flops 1342177280 | bytes 5242880 | tf_op jit(solution)/shard_map/pallas_call | solution.py:358
  159.5 4.6 %collective-permute-done.51 = bf16[64,2048]{1,0:T(8,128)(2,1)S(1)} collective-permute-done((bf16[64,2048]{1,0:T(8,128)(2,1)S(1)}, bf16[64,2048]{1,0:T(8,128)(2,1)S(1)}, u32[]{:S(2)}, u32[]{:S(2)}) %collective-permute-start.51) | collective-permute-done | bytes 262176 | tf_op jit(solution)/shard_map/ppermute | solution.py:34
  164.4 3.7 %collective-permute-start.54 = (bf16[2,16,2048]{2,1,0:T(8,128)(2,1)S(1)}, bf16[2,16,2048]{2,1,0:T(8,128)(2,1)S(1)}, u32[]{:S(2)}, u32[]{:S(2)}) collective-permute-start(bf16[2,16,2048]{2,1,0:T(8,128)(2,1)S(1)} %get-tuple-element.144), channel_id=1, source_target_pairs={{0,4},{4,0},{8,12},{12,8},{1,5},{5,1},{9,13},{13,9},{2,6},{6,2},{1... | collective-permute-start | bytes 393224 | tf_op jit(solution)/shard_map/ppermute | solution.py:34
  171.1 4.3 %shard_map.143 = (bf16[128,2048]{1,0:T(8,128)(2,1)S(1)}, bf16[128,2048]{1,0:T(8,128)(2,1)S(1)}) custom-call(f32[1280]{0:T(1024)S(1)} %copy-done.5, s32[1,256]{1,0:T(1,128)S(1)} %get-tuple-element.152.goes_ref, bf16[1280,2048]{1,0:T(8,128)(2,1)} %w_hbm.7, f32[128,1280]{1,0:T(8,128)S(1)} %bitcast.155, f32[128,1280]{1,0:T(8,128)S(1)} %bitcast.159), custom_call_target="tpu_custom_call" | custom-call | flops 1342177280 | bytes 5242880 | tf_op jit(solution)/shard_map/pallas_call | solution.py:358
  181.4 5.3 %collective-permute-done.56 = bf16[2,16,2048]{2,1,0:T(8,128)(2,1)S(1)} collective-permute-done((bf16[2,16,2048]{2,1,0:T(8,128)(2,1)S(1)}, bf16[2,16,2048]{2,1,0:T(8,128)(2,1)S(1)}, u32[]{:S(2)}, u32[]{:S(2)}) %collective-permute-start.56) | collective-permute-done | bytes 131104 | tf_op jit(solution)/shard_map/ppermute | solution.py:34
  196.1 7.1 %collective-permute-done.60 = bf16[2,16,2048]{2,1,0:T(8,128)(2,1)S(1)} collective-permute-done((bf16[2,16,2048]{2,1,0:T(8,128)(2,1)S(1)}, bf16[2,16,2048]{2,1,0:T(8,128)(2,1)S(1)}, u32[]{:S(2)}, u32[]{:S(2)}) %collective-permute-start.60) | collective-permute-done | bytes 131104 | tf_op jit(solution)/shard_map/ppermute | solution.py:34
  205.2 4.5 %collective-permute-done.65 = bf16[1,32,2048]{2,1,0:T(8,128)(2,1)S(1)} collective-permute-done((bf16[1,32,2048]{2,1,0:T(8,128)(2,1)S(1)}, bf16[1,32,2048]{2,1,0:T(8,128)(2,1)S(1)}, u32[]{:S(2)}, u32[]{:S(2)}) %collective-permute-start.65) | collective-permute-done | bytes 131104 | tf_op jit(solution)/shard_map/ppermute | solution.py:34
  (215 shorter events, 95.5 us)
Async XLA Ops:
  0.0 22.2 %collective-permute-start.1 = (bf16[320,1280]{1,0:T(8,128)(2,1)}, bf16[320,1280]{1,0:T(8,128)(2,1)S(1)}, u32[]{:S(2)}, u32[]{:S(2)}) collective-permute-start(bf16[320,1280]{1,0:T(8,128)(2,1)} %rest_4_), channel_id=1, source_target_pairs={{0,2},{1,3},{2,0},{3,1},{4,6},{5,7},{6,4},{7,5},{8,10},{9,11},{10,... | collective-permute-start | bytes 2457608 | tf_op jit(solution)/shard_map/ppermute | solution.py:34
  17.2 20.2 %collective-permute-start.5 = (bf16[256,320]{1,0:T(8,128)(2,1)}, bf16[256,320]{1,0:T(8,128)(2,1)}, u32[]{:S(2)}, u32[]{:S(2)}) collective-permute-start(bf16[256,320]{1,0:T(8,128)(2,1)} %get-tuple-element.69), channel_id=1, source_target_pairs={{0,2},{1,3},{2,0},{3,1},{4,6},{5,7},{6,4},{7,5},{8,10},{9,11},{10,... | collective-permute-start | bytes 491528 | tf_op jit(solution)/shard_map/ppermute | solution.py:34
  17.3 20.1 %collective-permute-start.6 = (bf16[256,320]{1,0:T(8,128)(2,1)}, bf16[256,320]{1,0:T(8,128)(2,1)}, u32[]{:S(2)}, u32[]{:S(2)}) collective-permute-start(bf16[256,320]{1,0:T(8,128)(2,1)} %get-tuple-element.70), channel_id=1, source_target_pairs={{0,3},{1,2},{2,1},{3,0},{4,7},{5,6},{6,5},{7,4},{8,11},{9,10},{10,... | collective-permute-start | bytes 491528 | tf_op jit(solution)/shard_map/ppermute | solution.py:34
  45.7 13.5 %collective-permute-start.12 = (bf16[64,1280]{1,0:T(8,128)(2,1)}, bf16[64,1280]{1,0:T(8,128)(2,1)S(1)}, u32[]{:S(2)}, u32[]{:S(2)}) collective-permute-start(bf16[64,1280]{1,0:T(8,128)(2,1)} %get-tuple-element.76), channel_id=1, source_target_pairs={{0,8},{4,12},{8,0},{12,4},{1,9},{5,13},{9,1},{13,5},{2,10},{6,14},... | collective-permute-start | bytes 491528 | tf_op jit(solution)/shard_map/ppermute | solution.py:34
  46.4 12.8 %collective-permute-start.13 = (bf16[64,1280]{1,0:T(8,128)(2,1)}, bf16[64,1280]{1,0:T(8,128)(2,1)S(1)}, u32[]{:S(2)}, u32[]{:S(2)}) collective-permute-start(bf16[64,1280]{1,0:T(8,128)(2,1)} %get-tuple-element.77), channel_id=1, source_target_pairs={{0,12},{4,8},{8,4},{12,0},{1,13},{5,9},{9,5},{13,1},{2,14},{6,10},... | collective-permute-start | bytes 491528 | tf_op jit(solution)/shard_map/ppermute | solution.py:34
  78.8 12.5 %collective-permute-start.33 = (bf16[2,64,1280]{2,1,0:T(8,128)(2,1)S(1)}, bf16[2,64,1280]{2,1,0:T(8,128)(2,1)S(1)}, u32[]{:S(2)}, u32[]{:S(2)}) collective-permute-start(bf16[2,64,1280]{2,1,0:T(8,128)(2,1)S(1)} %slice_bitcast_fusion), channel_id=1, source_target_pairs={{12,8},{13,9},{14,10},{15,11},{28,24},{29,25},{30,26},{31,27}} | collective-permute-start | bytes 983048 | tf_op jit(solution)/shard_map/ppermute | solution.py:85
  79.6 14.2 %collective-permute-start.19 = (bf16[2,64,1280]{2,1,0:T(8,128)(2,1)S(1)}, bf16[2,64,1280]{2,1,0:T(8,128)(2,1)S(1)}, u32[]{:S(2)}, u32[]{:S(2)}) collective-permute-start(bf16[2,64,1280]{2,1,0:T(8,128)(2,1)S(1)} %fusion), channel_id=1, source_target_pairs={{0,4},{4,8},{1,5},{5,9},{2,6},{6,10},{3,7},{7,11},{16,20},{20,24},... | collective-permute-start | bytes 983048 | tf_op jit(solution)/shard_map/ppermute | solution.py:85
  83.2 15.1 %collective-permute-start.22 = (bf16[2,64,1280]{2,1,0:T(8,128)(2,1)S(1)}, bf16[2,64,1280]{2,1,0:T(8,128)(2,1)S(1)}, u32[]{:S(2)}, u32[]{:S(2)}) collective-permute-start(bf16[2,64,1280]{2,1,0:T(8,128)(2,1)S(1)} %fusion.4), channel_id=1, source_target_pairs={{12,8},{8,4},{13,9},{9,5},{14,10},{10,6},{15,11},{11,7},{28,24},{2... | collective-permute-start | bytes 983048 | tf_op jit(solution)/shard_map/ppermute | solution.py:85
  86.9 14.0 %collective-permute-start.31 = (bf16[2,64,1280]{2,1,0:T(8,128)(2,1)S(1)}, bf16[2,64,1280]{2,1,0:T(8,128)(2,1)S(1)}, u32[]{:S(2)}, u32[]{:S(2)}) collective-permute-start(bf16[2,64,1280]{2,1,0:T(8,128)(2,1)S(1)} %fusion.2), channel_id=1, source_target_pairs={{0,4},{4,8},{1,5},{5,9},{2,6},{6,10},{3,7},{7,11},{16,20},{20,24},... | collective-permute-start | bytes 983048 | tf_op jit(solution)/shard_map/ppermute | solution.py:85
  91.4 14.0 %collective-permute-start.34 = (bf16[2,64,1280]{2,1,0:T(8,128)(2,1)S(1)}, bf16[2,64,1280]{2,1,0:T(8,128)(2,1)S(1)}, u32[]{:S(2)}, u32[]{:S(2)}) collective-permute-start(bf16[2,64,1280]{2,1,0:T(8,128)(2,1)S(1)} %fusion.10), channel_id=1, source_target_pairs={{12,8},{8,4},{13,9},{9,5},{14,10},{10,6},{15,11},{11,7},{28,24},{2... | collective-permute-start | bytes 983048 | tf_op jit(solution)/shard_map/ppermute | solution.py:85
  93.9 14.0 %collective-permute-start.20 = (bf16[2,64,1280]{2,1,0:T(8,128)(2,1)S(1)}, bf16[2,64,1280]{2,1,0:T(8,128)(2,1)S(1)}, u32[]{:S(2)}, u32[]{:S(2)}) collective-permute-start(bf16[2,64,1280]{2,1,0:T(8,128)(2,1)S(1)} %fusion.6), channel_id=1, source_target_pairs={{0,4},{4,8},{8,12},{1,5},{5,9},{9,13},{2,6},{6,10},{10,14},{3,7},{... | collective-permute-start | bytes 983048 | tf_op jit(solution)/shard_map/ppermute | solution.py:85
  101.0 14.0 %collective-permute-start.32 = (bf16[2,64,1280]{2,1,0:T(8,128)(2,1)S(1)}, bf16[2,64,1280]{2,1,0:T(8,128)(2,1)S(1)}, u32[]{:S(2)}, u32[]{:S(2)}) collective-permute-start(bf16[2,64,1280]{2,1,0:T(8,128)(2,1)S(1)} %fusion.12), channel_id=1, source_target_pairs={{0,4},{4,8},{8,12},{1,5},{5,9},{9,13},{2,6},{6,10},{10,14},{3,7},{... | collective-permute-start | bytes 983048 | tf_op jit(solution)/shard_map/ppermute | solution.py:85
  108.6 13.6 %collective-permute-start.36 = (bf16[2,64,1280]{2,1,0:T(8,128)(2,1)S(1)}, bf16[2,64,1280]{2,1,0:T(8,128)(2,1)S(1)}, u32[]{:S(2)}, u32[]{:S(2)}) collective-permute-start(bf16[2,64,1280]{2,1,0:T(8,128)(2,1)S(1)} %get-tuple-element.126), channel_id=1, source_target_pairs={{0,4},{4,8},{8,12},{1,5},{5,9},{9,13},{2,6},{6,10},{10,14},{3,7},{... | collective-permute-start | bytes 983048 | tf_op jit(solution)/shard_map/ppermute | solution.py:85
  112.7 12.7 %collective-permute-start.37 = (bf16[2,64,1280]{2,1,0:T(8,128)(2,1)S(1)}, bf16[2,64,1280]{2,1,0:T(8,128)(2,1)S(1)}, u32[]{:S(2)}, u32[]{:S(2)}) collective-permute-start(bf16[2,64,1280]{2,1,0:T(8,128)(2,1)S(1)} %get-tuple-element.151), channel_id=1, source_target_pairs={{12,8},{8,4},{4,0},{13,9},{9,5},{5,1},{14,10},{10,6},{6,2},{15,11}... | collective-permute-start | bytes 983048 | tf_op jit(solution)/shard_map/ppermute | solution.py:85
  115.6 16.8 %collective-permute-start.42 = (bf16[2,64,1280]{2,1,0:T(8,128)(2,1)S(1)}, bf16[2,64,1280]{2,1,0:T(8,128)(2,1)S(1)}, u32[]{:S(2)}, u32[]{:S(2)}) collective-permute-start(bf16[2,64,1280]{2,1,0:T(8,128)(2,1)S(1)} %get-tuple-element.124), channel_id=1, source_target_pairs={{0,4},{4,8},{8,12},{1,5},{5,9},{9,13},{2,6},{6,10},{10,14},{3,7},{... | collective-permute-start | bytes 983048 | tf_op jit(solution)/shard_map/ppermute | solution.py:85
  126.5 13.0 %collective-permute-start.41 = (bf16[2,64,1280]{2,1,0:T(8,128)(2,1)S(1)}, bf16[2,64,1280]{2,1,0:T(8,128)(2,1)S(1)}, u32[]{:S(2)}, u32[]{:S(2)}) collective-permute-start(bf16[2,64,1280]{2,1,0:T(8,128)(2,1)S(1)} %get-tuple-element.150), channel_id=1, source_target_pairs={{8,4},{4,0},{9,5},{5,1},{10,6},{6,2},{11,7},{7,3},{24,20},{20,16},... | collective-permute-start | bytes 983048 | tf_op jit(solution)/shard_map/ppermute | solution.py:85
  133.3 14.5 %collective-permute-start.45 = (bf16[2,64,1280]{2,1,0:T(8,128)(2,1)S(1)}, bf16[2,64,1280]{2,1,0:T(8,128)(2,1)S(1)}, u32[]{:S(2)}, u32[]{:S(2)}) collective-permute-start(bf16[2,64,1280]{2,1,0:T(8,128)(2,1)S(1)} %add_convert_fusion.4), channel_id=1, source_target_pairs={{8,4},{4,0},{9,5},{5,1},{10,6},{6,2},{11,7},{7,3},{24,20},{20,16},... | collective-permute-start | bytes 983048 | tf_op jit(solution)/shard_map/ppermute | solution.py:85
  135.0 12.9 %collective-permute-start.43 = (bf16[2,64,1280]{2,1,0:T(8,128)(2,1)S(1)}, bf16[2,64,1280]{2,1,0:T(8,128)(2,1)S(1)}, u32[]{:S(2)}, u32[]{:S(2)}) collective-permute-start(bf16[2,64,1280]{2,1,0:T(8,128)(2,1)S(1)} %get-tuple-element.118), channel_id=1, source_target_pairs={{4,8},{8,12},{5,9},{9,13},{6,10},{10,14},{7,11},{11,15},{20,24},{2... | collective-permute-start | bytes 983048 | tf_op jit(solution)/shard_map/ppermute | solution.py:85
  140.6 14.2 %collective-permute-start.47 = (bf16[2,64,1280]{2,1,0:T(8,128)(2,1)S(1)}, bf16[2,64,1280]{2,1,0:T(8,128)(2,1)S(1)}, u32[]{:S(2)}, u32[]{:S(2)}) collective-permute-start(bf16[2,64,1280]{2,1,0:T(8,128)(2,1)S(1)} %get-tuple-element.148), channel_id=1, source_target_pairs={{4,0},{5,1},{6,2},{7,3},{20,16},{21,17},{22,18},{23,19}} | collective-permute-start | bytes 983048 | tf_op jit(solution)/shard_map/ppermute | solution.py:85
  147.9 16.3 %collective-permute-start.50 = (bf16[2,64,1280]{2,1,0:T(8,128)(2,1)S(1)}, bf16[2,64,1280]{2,1,0:T(8,128)(2,1)S(1)}, u32[]{:S(2)}, u32[]{:S(2)}) collective-permute-start(bf16[2,64,1280]{2,1,0:T(8,128)(2,1)S(1)} %fusion.11), channel_id=1, source_target_pairs={{4,0},{5,1},{6,2},{7,3},{20,16},{21,17},{22,18},{23,19}} | collective-permute-start | bytes 983048 | tf_op jit(solution)/shard_map/ppermute | solution.py:85
  149.5 14.6 %collective-permute-start.49 = (bf16[2,64,1280]{2,1,0:T(8,128)(2,1)S(1)}, bf16[2,64,1280]{2,1,0:T(8,128)(2,1)S(1)}, u32[]{:S(2)}, u32[]{:S(2)}) collective-permute-start(bf16[2,64,1280]{2,1,0:T(8,128)(2,1)S(1)} %get-tuple-element.116), channel_id=1, source_target_pairs={{8,12},{9,13},{10,14},{11,15},{24,28},{25,29},{26,30},{27,31}} | collective-permute-start | bytes 983048 | tf_op jit(solution)/shard_map/ppermute | solution.py:85
  150.5 13.8 %collective-permute-start.39 = (bf16[64,2048]{1,0:T(8,128)(2,1)S(1)}, bf16[64,2048]{1,0:T(8,128)(2,1)S(1)}, u32[]{:S(2)}, u32[]{:S(2)}) collective-permute-start(bf16[64,2048]{1,0:T(8,128)(2,1)S(1)} %slice.139), channel_id=1, source_target_pairs={{0,2},{1,3},{2,0},{3,1},{4,6},{5,7},{6,4},{7,5},{8,10},{9,11},{10,... | collective-permute-start | bytes 786440 | tf_op jit(solution)/shard_map/ppermute | solution.py:34
  151.1 12.9 %collective-permute-start.51 = (bf16[64,2048]{1,0:T(8,128)(2,1)S(1)}, bf16[64,2048]{1,0:T(8,128)(2,1)S(1)}, u32[]{:S(2)}, u32[]{:S(2)}) collective-permute-start(bf16[64,2048]{1,0:T(8,128)(2,1)S(1)} %slice.141), channel_id=1, source_target_pairs={{0,2},{1,3},{2,0},{3,1},{4,6},{5,7},{6,4},{7,5},{8,10},{9,11},{10,... | collective-permute-start | bytes 786440 | tf_op jit(solution)/shard_map/ppermute | solution.py:34
  164.4 14.4 %collective-permute-start.54 = (bf16[2,16,2048]{2,1,0:T(8,128)(2,1)S(1)}, bf16[2,16,2048]{2,1,0:T(8,128)(2,1)S(1)}, u32[]{:S(2)}, u32[]{:S(2)}) collective-permute-start(bf16[2,16,2048]{2,1,0:T(8,128)(2,1)S(1)} %get-tuple-element.144), channel_id=1, source_target_pairs={{0,4},{4,0},{8,12},{12,8},{1,5},{5,1},{9,13},{13,9},{2,6},{6,2},{1... | collective-permute-start | bytes 393224 | tf_op jit(solution)/shard_map/ppermute | solution.py:34
  (57 other events, 527.9 us)
